TPU v7x, 32 devices: a whole 2x2x4 slice. The times are simulated.
32 devices in a mesh: section: 2 (over core), dp: 4 (over z), replica: 4 (over y, x).
Axes of the slice: x: 2, y: 2, z: 4, core: 2. Of those that a mesh axis runs over, the one named last changes fastest.
Arguments:
- tokens: bfloat16 [16384, 768], P(('dp', 'replica')), may hold values from -6 to 6
- cotangent: bfloat16 [16384, 768], P(('dp', 'replica')), may hold values from -6 to 6
- lengths: int32 [32], P(('dp', 'replica')), may hold values from 100 to 512, as said below
- attn_gain: bfloat16 [2, 768], P('section'), may hold values from 0.25 to 1.75
- attn_shift: bfloat16 [2, 768], P('section'), may hold values from -1.5 to 1.5
- qkv_weight: bfloat16 [2, 768, 2304], P('section'), may hold values from -0.3125 to 0.3125
- qkv_bias: bfloat16 [2, 2304], P('section'), may hold values from -1.5 to 1.5
- out_weight: bfloat16 [2, 768, 768], P('section'), may hold values from -0.625 to 0.625
- out_bias: bfloat16 [2, 768], P('section'), may hold values from -1.5 to 1.5
- mlp_gain: bfloat16 [2, 768], P('section'), may hold values from 0.25 to 1.75
- mlp_shift: bfloat16 [2, 768], P('section'), may hold values from -1.5 to 1.5
- up_weight: bfloat16 [2, 768, 3072], P('section'), may hold values from -0.21875 to 0.21875
- up_bias: bfloat16 [2, 3072], P('section'), may hold values from -2.5 to 2.5
- down_weight: bfloat16 [2, 3072, 768], P('section'), may hold values from -0.109375 to 0.109375
- down_bias: bfloat16 [2, 768], P('section'), may hold values from -1.5 to 1.5
Outputs:
- block_outputs: bfloat16 [2, 16384, 768], P('section', ('dp', 'replica'))
- input_grads: float32 [2, 16384, 768], P('section', ('dp', 'replica'))
- grad_attn_gain: float32 [2, 768], P('section', 'dp')
- grad_attn_shift: float32 [2, 768], P('section', 'dp')
- grad_qkv_weight: float32 [2, 768, 2304], P('section', 'dp')
- grad_qkv_bias: float32 [2, 2304], P('section', 'dp')
- grad_out_weight: float32 [2, 768, 768], P('section', 'dp')
- grad_out_bias: float32 [2, 768], P('section', 'dp')
- grad_mlp_gain: float32 [2, 768], P('section', 'dp')
- grad_mlp_shift: float32 [2, 768], P('section', 'dp')
- grad_up_weight: float32 [2, 768, 3072], P('section', 'dp')
- grad_up_bias: float32 [2, 3072], P('section', 'dp')
- grad_down_weight: float32 [2, 3072, 768], P('section', 'dp')
- grad_down_bias: float32 [2, 768], P('section', 'dp')
Inputs may be any that keep to these rules, and one draw needn't show every extreme that they name: `lengths`: some sentence has exactly 512 genes and another exactly 100.
All inputs are finite; a program needn't handle non-finite values.
Results may differ from a plain program's by a relative error of at most 0.03.
The roundings to bfloat16 on the way count: a program that leaves them out, or rounds other values in their place, can miss the bound.
Values may be sent and summed in bfloat16 or wider, within the bound.
A program may use at most 256 MiB of HBM per device.

v0:
```python
import jax
import jax.numpy as jnp
from jax import lax
from jax.sharding import PartitionSpec as P

HEADS = 12
HEAD_DIM = 64
ROTARY = 16


EPSILON = 1e-05
ROTARY_BASE = 10000.0
MASKED = -1e30


def shifted_2(value, axis, by):
    size = lax.axis_size(axis)
    pairs = [(i, i + by) for i in range(size) if 0 <= i + by < size]
    return lax.ppermute(value, axis, pairs)


def rotary_tables(seq_len):
    positions = jnp.arange(seq_len, dtype=jnp.float32)
    inverse = 1.0 / ROTARY_BASE ** (jnp.arange(0, ROTARY, 2, dtype=jnp.float32) / ROTARY)
    angles = positions[:, None] * inverse[None, :]
    angles = jnp.concatenate([angles, angles], axis=-1)
    return (jnp.cos(angles), jnp.sin(angles))


def rotate(per_head, cosine_tab, sine_tab):
    half_rot = ROTARY // 2
    turning = per_head[..., :ROTARY]
    swapped = jnp.concatenate([-turning[..., half_rot:], turning[..., :half_rot]], axis=-1)
    turned = turning * cosine_tab[:, None, :] + swapped * sine_tab[:, None, :]
    return jnp.concatenate([turned, per_head[..., ROTARY:]], axis=-1)


def unrotate(grad_head, cosine_tab, sine_tab):
    half_rot = ROTARY // 2
    turning = grad_head[..., :ROTARY]
    along_cos = turning * cosine_tab[:, None, :]
    along_sin = turning * sine_tab[:, None, :]
    back_turn = along_cos + jnp.concatenate(
        [along_sin[..., half_rot:], -along_sin[..., :half_rot]], axis=-1
    )
    return jnp.concatenate([back_turn, grad_head[..., ROTARY:]], axis=-1)


def normalize(block_in):
    centre = jnp.mean(block_in, axis=-1, keepdims=True)
    centred = block_in - centre
    inv_spread = lax.rsqrt(jnp.mean(centred * centred, axis=-1, keepdims=True) + EPSILON)
    return (centred * inv_spread, inv_spread)


def score_block(query_blk, keys_rot, length):
    raw_scores = jnp.einsum(
        "qhd,khd->hqk", query_blk, keys_rot, preferred_element_type=jnp.float32
    ) * HEAD_DIM ** (-0.5)
    row_ids = jnp.arange(query_blk.shape[0])[:, None]
    col_ids = jnp.arange(keys_rot.shape[0])[None, :]
    allowed = (col_ids <= row_ids) & (col_ids < length)
    return jnp.where(allowed[None], raw_scores, MASKED)


def layer_forward(block_in, length, weights, cosine_tab, sine_tab):
    (
        attn_gain,
        attn_shift,
        qkv_weight,
        qkv_bias,
        out_weight,
        out_bias,
        mlp_gain,
        mlp_shift,
        up_weight,
        up_bias,
        down_weight,
        down_bias,
    ) = weights
    seq_len, model_width = block_in.shape
    unit_rows, inv_spread = normalize(block_in)
    attn_in = (unit_rows * attn_gain + attn_shift).astype(jnp.bfloat16)
    projected = jnp.dot(attn_in, qkv_weight, preferred_element_type=jnp.float32) + qkv_bias
    projected = projected.reshape(seq_len, 3, HEADS, HEAD_DIM)
    queries = rotate(projected[:, 0], cosine_tab, sine_tab).astype(jnp.bfloat16)
    keys_rot = rotate(projected[:, 1], cosine_tab, sine_tab).astype(jnp.bfloat16)
    values_in = projected[:, 2].astype(jnp.bfloat16)
    scores = score_block(queries, keys_rot, length)
    highest = jnp.max(scores, axis=-1, keepdims=True)
    shifted = jnp.exp(scores - highest)
    row_total = jnp.sum(shifted, axis=-1, keepdims=True)
    probs_low = (shifted / row_total).astype(jnp.bfloat16)
    contexts = [
        jnp.einsum("hqk,khd->qhd", probs_low, values_in, preferred_element_type=jnp.float32)
    ]
    totals = [highest + jnp.log(row_total)]
    context = jnp.concatenate(contexts, axis=0).reshape(seq_len, model_width).astype(jnp.bfloat16)
    log_total = jnp.concatenate(totals, axis=1)
    attn_out = jnp.dot(context, out_weight, preferred_element_type=jnp.float32) + out_bias
    mlp_in = (unit_rows * mlp_gain + mlp_shift).astype(jnp.bfloat16)
    up_pre = jnp.dot(mlp_in, up_weight, preferred_element_type=jnp.float32) + up_bias
    hidden = jax.nn.gelu(up_pre, approximate=False).astype(jnp.bfloat16)
    mlp_out = jnp.dot(hidden, down_weight, preferred_element_type=jnp.float32) + down_bias
    block_out = block_in + attn_out + mlp_out
    saved_vals = (
        unit_rows,
        inv_spread,
        attn_in,
        mlp_in,
        queries,
        keys_rot,
        values_in,
        log_total,
        context,
        up_pre,
        hidden,
    )
    return (block_out, saved_vals)


def layer_backward(grad_out, length, weights, saved_vals, cosine_tab, sine_tab):
    (
        attn_gain,
        attn_shift,
        qkv_weight,
        qkv_bias,
        out_weight,
        out_bias,
        mlp_gain,
        mlp_shift,
        up_weight,
        up_bias,
        down_weight,
        down_bias,
    ) = weights
    (
        unit_rows,
        inv_spread,
        attn_in,
        mlp_in,
        queries,
        keys_rot,
        values_in,
        log_total,
        context,
        up_pre,
        hidden,
    ) = saved_vals
    seq_len, model_width = grad_out.shape
    grad_wide = grad_out.astype(jnp.float32)
    grad_down_weight = jnp.einsum("rf,rd->fd", hidden, grad_out, preferred_element_type=jnp.float32)
    bias_sum = jnp.sum(grad_wide, axis=0)
    grad_hidden = jnp.einsum("rd,fd->rf", grad_out, down_weight, preferred_element_type=jnp.float32)
    gelu_value, gelu_back = jax.vjp(lambda pre_act: jax.nn.gelu(pre_act, approximate=False), up_pre)
    grad_up_pre = gelu_back(grad_hidden)[0].astype(jnp.bfloat16)
    grad_up_weight = jnp.einsum(
        "rd,rf->df", mlp_in, grad_up_pre, preferred_element_type=jnp.float32
    )
    grad_up_bias = jnp.sum(grad_up_pre.astype(jnp.float32), axis=0)
    grad_mlp_in = jnp.einsum(
        "rf,df->rd", grad_up_pre, up_weight, preferred_element_type=jnp.float32
    )
    grad_out_weight = jnp.einsum("re,rd->ed", context, grad_out, preferred_element_type=jnp.float32)
    grad_context = jnp.einsum("rd,ed->re", grad_out, out_weight, preferred_element_type=jnp.float32)
    grad_context = grad_context.astype(jnp.bfloat16).reshape(seq_len, HEADS, HEAD_DIM)
    score_scale = HEAD_DIM ** (-0.5)
    scores = score_block(queries, keys_rot, length)
    probs_blk = jnp.exp(scores - log_total)
    grad_probs = jnp.einsum(
        "qhd,khd->hqk", grad_context, values_in, preferred_element_type=jnp.float32
    )
    grad_values = jnp.einsum(
        "hqk,qhd->khd",
        probs_blk.astype(jnp.bfloat16),
        grad_context,
        preferred_element_type=jnp.float32,
    )
    inner_sum = jnp.sum(probs_blk * grad_probs, axis=-1, keepdims=True)
    grad_scores = (probs_blk * (grad_probs - inner_sum)).astype(jnp.bfloat16)
    query_parts = [
        jnp.einsum("hqk,khd->qhd", grad_scores, keys_rot, preferred_element_type=jnp.float32)
        * score_scale
    ]
    grad_keys = (
        jnp.einsum("hqk,qhd->khd", grad_scores, queries, preferred_element_type=jnp.float32)
        * score_scale
    )
    grad_queries = jnp.concatenate(query_parts, axis=0)
    grad_projected = jnp.stack(
        [
            unrotate(grad_queries, cosine_tab, sine_tab),
            unrotate(grad_keys, cosine_tab, sine_tab),
            grad_values,
        ],
        axis=1,
    )
    grad_projected = grad_projected.reshape(seq_len, 3 * model_width).astype(jnp.bfloat16)
    grad_qkv_weight = jnp.einsum(
        "rd,re->de", attn_in, grad_projected, preferred_element_type=jnp.float32
    )
    grad_qkv_bias = jnp.sum(grad_projected.astype(jnp.float32), axis=0)
    grad_attn_in = jnp.einsum(
        "re,de->rd", grad_projected, qkv_weight, preferred_element_type=jnp.float32
    )
    grad_attn_gain = jnp.sum(grad_attn_in * unit_rows, axis=0)
    grad_attn_shift = jnp.sum(grad_attn_in, axis=0)
    grad_mlp_gain = jnp.sum(grad_mlp_in * unit_rows, axis=0)
    grad_mlp_shift = jnp.sum(grad_mlp_in, axis=0)
    grad_unit = grad_attn_in * attn_gain + grad_mlp_in * mlp_gain
    grad_in = grad_wide + inv_spread * (
        grad_unit
        - jnp.mean(grad_unit, axis=-1, keepdims=True)
        - unit_rows * jnp.mean(grad_unit * unit_rows, axis=-1, keepdims=True)
    )
    layer_grads = (
        grad_attn_gain,
        grad_attn_shift,
        grad_qkv_weight,
        grad_qkv_bias,
        grad_out_weight,
        bias_sum,
        grad_mlp_gain,
        grad_mlp_shift,
        grad_up_weight,
        grad_up_bias,
        grad_down_weight,
        bias_sum,
    )
    return (grad_in, layer_grads)


def stash_zeros(micro_count, seq_len, model_width, hidden_width):
    return (
        jnp.zeros((micro_count, seq_len, model_width), jnp.float32),
        jnp.zeros((micro_count, seq_len, 1), jnp.float32),
        jnp.zeros((micro_count, seq_len, model_width), jnp.bfloat16),
        jnp.zeros((micro_count, seq_len, model_width), jnp.bfloat16),
        jnp.zeros((micro_count, seq_len, HEADS, HEAD_DIM), jnp.bfloat16),
        jnp.zeros((micro_count, seq_len, HEADS, HEAD_DIM), jnp.bfloat16),
        jnp.zeros((micro_count, seq_len, HEADS, HEAD_DIM), jnp.bfloat16),
        jnp.zeros((micro_count, HEADS, seq_len, 1), jnp.float32),
        jnp.zeros((micro_count, seq_len, model_width), jnp.bfloat16),
        jnp.zeros((micro_count, seq_len, hidden_width), jnp.float32),
        jnp.zeros((micro_count, seq_len, hidden_width), jnp.bfloat16),
    )


def body(
    tokens,
    cotangent,
    lengths,
    attn_gain,
    attn_shift,
    qkv_weight,
    qkv_bias,
    out_weight,
    out_bias,
    mlp_gain,
    mlp_shift,
    up_weight,
    up_bias,
    down_weight,
    down_bias,
):
    weights = tuple(
        (
            weight_arr[0]
            for weight_arr in (
                attn_gain,
                attn_shift,
                qkv_weight,
                qkv_bias,
                out_weight,
                out_bias,
                mlp_gain,
                mlp_shift,
                up_weight,
                up_bias,
                down_weight,
                down_bias,
            )
        )
    )
    micro_count = lengths.shape[0]
    seq_len = tokens.shape[0] // micro_count
    model_width = tokens.shape[1]
    hidden_width = weights[8].shape[1]
    section_index = lax.axis_index("section")
    is_first = section_index == 0
    inputs = tokens.reshape(micro_count, seq_len, model_width)
    cotans = cotangent.reshape(micro_count, seq_len, model_width)
    cosine_tab, sine_tab = rotary_tables(seq_len)
    empty_rows = jnp.zeros((seq_len, model_width), jnp.bfloat16)
    row_ids = jnp.arange(seq_len)[:, None]

    def forward_only(block_low, length):
        return layer_forward(block_low.astype(jnp.float32), length, weights, cosine_tab, sine_tab)

    stash_all = stash_zeros(micro_count, seq_len, model_width, hidden_width)

    def forward_step(block_low, length, slot_index, outputs, stash_now):
        block_out, saved_vals = forward_only(block_low, length)
        out_low = block_out.astype(jnp.bfloat16)
        outputs = lax.dynamic_update_index_in_dim(outputs, out_low, slot_index, 0)
        stash_now = jax.tree.map(
            lambda buffer, newest: lax.dynamic_update_index_in_dim(buffer, newest, slot_index, 0),
            stash_now,
            saved_vals,
        )
        return (out_low, outputs, stash_now)

    def forward_spare(block_low, length, slot_index, outputs, stash_now):
        return (empty_rows, outputs, stash_now)

    received = empty_rows
    outputs = jnp.zeros((micro_count, seq_len, model_width), jnp.bfloat16)
    for moment in range(micro_count + 1):
        index_now = moment - section_index
        active = (index_now >= 0) & (index_now < micro_count)
        slot_index = jnp.clip(index_now, 0, micro_count - 1)
        length = lax.dynamic_index_in_dim(lengths, slot_index, 0, keepdims=False)
        own_rows = lax.dynamic_index_in_dim(inputs, slot_index, 0, keepdims=False)
        block_low = jnp.where(is_first, own_rows, received)
        out_low, outputs, stash_all = lax.cond(
            active, forward_step, forward_spare, block_low, length, slot_index, outputs, stash_all
        )
        if moment < micro_count:
            received = shifted_2(out_low, "section", 1)

    def backward_step(grad_low, length, slot_index, totals, grad_rows):
        stored = jax.tree.map(
            lambda buffer: lax.dynamic_index_in_dim(buffer, slot_index, 0, keepdims=False),
            stash_all,
        )
        grad_in, layer_grads = layer_backward(
            grad_low, length, weights, stored, cosine_tab, sine_tab
        )
        grad_low_in = grad_in.astype(jnp.bfloat16)
        reported = jnp.where(is_first, grad_in, grad_low_in.astype(jnp.float32))
        grad_rows = lax.dynamic_update_index_in_dim(grad_rows, reported, slot_index, 0)
        totals = jax.tree.map(jnp.add, totals, layer_grads)
        return (grad_low_in, totals, grad_rows)

    def backward_spare(grad_low, length, slot_index, totals, grad_rows):
        return (empty_rows, totals, grad_rows)

    back_in = empty_rows
    totals = tuple((jnp.zeros(weight_arr.shape, jnp.float32) for weight_arr in weights))
    grad_rows = jnp.zeros((micro_count, seq_len, model_width), jnp.float32)
    for moment in range(micro_count + 1):
        index_now = moment - 1 + section_index
        active = (index_now >= 0) & (index_now < micro_count)
        slot_index = jnp.clip(index_now, 0, micro_count - 1)
        length = lax.dynamic_index_in_dim(lengths, slot_index, 0, keepdims=False)
        own_cot = lax.dynamic_index_in_dim(cotans, slot_index, 0, keepdims=False)
        own_cot = jnp.where(row_ids < length, own_cot, jnp.zeros_like(own_cot))
        grad_low = jnp.where(is_first, back_in, own_cot)
        grad_send, totals, grad_rows = lax.cond(
            active, backward_step, backward_spare, grad_low, length, slot_index, totals, grad_rows
        )
        if moment < micro_count:
            back_in = shifted_2(grad_send, "section", -1)
    (
        sum_attn_gain,
        sum_attn_shift,
        sum_qkv_weight,
        sum_qkv_bias,
        sum_out_weight,
        sum_out_bias,
        sum_mlp_gain,
        sum_mlp_shift,
        sum_up_weight,
        sum_up_bias,
        sum_down_weight,
        sum_down_bias,
    ) = totals
    shares = (
        lax.psum_scatter(
            sum_attn_gain.astype(jnp.bfloat16), "dp", scatter_dimension=0, tiled=True
        ).astype(jnp.float32),
        lax.psum_scatter(
            sum_attn_shift.astype(jnp.bfloat16), "dp", scatter_dimension=0, tiled=True
        ).astype(jnp.float32),
        lax.psum_scatter(
            sum_qkv_weight.astype(jnp.bfloat16), "dp", scatter_dimension=0, tiled=True
        ).astype(jnp.float32),
        lax.psum_scatter(
            sum_qkv_bias.astype(jnp.bfloat16), "dp", scatter_dimension=0, tiled=True
        ).astype(jnp.float32),
        lax.psum_scatter(
            sum_out_weight.astype(jnp.bfloat16), "dp", scatter_dimension=0, tiled=True
        ).astype(jnp.float32),
        lax.psum_scatter(
            sum_out_bias.astype(jnp.bfloat16), "dp", scatter_dimension=0, tiled=True
        ).astype(jnp.float32),
        lax.psum_scatter(
            sum_mlp_gain.astype(jnp.bfloat16), "dp", scatter_dimension=0, tiled=True
        ).astype(jnp.float32),
        lax.psum_scatter(
            sum_mlp_shift.astype(jnp.bfloat16), "dp", scatter_dimension=0, tiled=True
        ).astype(jnp.float32),
        lax.psum_scatter(
            sum_up_weight.astype(jnp.bfloat16), "dp", scatter_dimension=0, tiled=True
        ).astype(jnp.float32),
        lax.psum_scatter(
            sum_up_bias.astype(jnp.bfloat16), "dp", scatter_dimension=0, tiled=True
        ).astype(jnp.float32),
        lax.psum_scatter(
            sum_down_weight.astype(jnp.bfloat16), "dp", scatter_dimension=0, tiled=True
        ).astype(jnp.float32),
        lax.psum_scatter(
            sum_down_bias.astype(jnp.bfloat16), "dp", scatter_dimension=0, tiled=True
        ).astype(jnp.float32),
    )
    shares = (
        lax.psum(shares[0].astype(jnp.bfloat16), "replica").astype(jnp.float32),
        lax.psum(shares[1].astype(jnp.bfloat16), "replica").astype(jnp.float32),
        lax.psum(shares[2].astype(jnp.bfloat16), "replica").astype(jnp.float32),
        lax.psum(shares[3].astype(jnp.bfloat16), "replica").astype(jnp.float32),
        lax.psum(shares[4].astype(jnp.bfloat16), "replica").astype(jnp.float32),
        lax.psum(shares[5].astype(jnp.bfloat16), "replica").astype(jnp.float32),
        lax.psum(shares[6].astype(jnp.bfloat16), "replica").astype(jnp.float32),
        lax.psum(shares[7].astype(jnp.bfloat16), "replica").astype(jnp.float32),
        lax.psum(shares[8].astype(jnp.bfloat16), "replica").astype(jnp.float32),
        lax.psum(shares[9].astype(jnp.bfloat16), "replica").astype(jnp.float32),
        lax.psum(shares[10].astype(jnp.bfloat16), "replica").astype(jnp.float32),
        lax.psum(shares[11].astype(jnp.bfloat16), "replica").astype(jnp.float32),
    )
    grad_scale = float(tokens.shape[0] * lax.axis_size("dp") * lax.axis_size("replica")) ** (-0.5)
    scaled = tuple((share_arr[None] * grad_scale for share_arr in shares))
    return (
        outputs.reshape(micro_count * seq_len, model_width)[None],
        grad_rows.reshape(micro_count * seq_len, model_width)[None],
        scaled[0],
        scaled[1],
        scaled[2],
        scaled[3],
        scaled[4],
        scaled[5],
        scaled[6],
        scaled[7],
        scaled[8],
        scaled[9],
        scaled[10],
        scaled[11],
    )


def solution(mesh):
    return jax.shard_map(
        body,
        mesh=mesh,
        in_specs=(
            P(("dp", "replica"), None),
            P(("dp", "replica"), None),
            P(("dp", "replica")),
            P("section", None),
            P("section", None),
            P("section", None, None),
            P("section", None),
            P("section", None, None),
            P("section", None),
            P("section", None),
            P("section", None),
            P("section", None, None),
            P("section", None),
            P("section", None, None),
            P("section", None),
        ),
        out_specs=(
            P("section", ("dp", "replica"), None),
            P("section", ("dp", "replica"), None),
            P("section", "dp"),
            P("section", "dp"),
            P("section", "dp", None),
            P("section", "dp"),
            P("section", "dp", None),
            P("section", "dp"),
            P("section", "dp"),
            P("section", "dp"),
            P("section", "dp", None),
            P("section", "dp"),
            P("section", "dp", None),
            P("section", "dp"),
        ),
        check_vma=False,
    )
```

profile of v0, /device:TPU:0, one launch (start us, length us, event | category | flops | bytes accessed | tf_op | source)
XLA Modules:
  0.0 983.7 jit_solution(6873357078797676901)
XLA Ops:
  17.7 92.0 %conditional.6 = (bf16[512,768]{1,0:T(8,128)(2,1)}, bf16[2,512,768]{2,1,0:T(8,128)(2,1)}, f32[2,512,768]{2,1,0:T(8,128)}, f32[2,512,1]{1,2,0:T(1,128)}, bf16[2,5...) conditional(s32[]{:T(128)} %convert_element_type.808, () %tuple.97, ...), branch_computations={%region_0.1_spmd, %region_1.6_spmd} | conditional | flops 8221399040 | bytes 233252576 | solution.py:325
  21.2 6.3 convolution_add_fusion
  27.5 6.6 copy.88
  40.4 3.5 fusion.1
  46.9 6.4 fusion.26
  58.3 3.3 broadcast_in_dim.398
  61.7 19.1 %bitcast_dynamic-update-slice_fusion.1 = (bf16[2,512,3072]{2,1,0:T(8,128)(2,1)}, bf16[512,3072]{1,0:T(8,128)(2,1)S(1)}, f32[512,3072]{1,0:T(8,128)S(1)}) fusion(bf16[2,512,3072]{2,1,0:T(8,128)(2,1)} %broadcast_in_dim.398, s32[]{:T(128)S(6)} %min.19, f32[3072]{0:T(1024)S(1)} %convert_element_type.689, bf16[768,3072]{1,0:T(8,128)(2,1)} %get-tuple-element.1651, ...), kind=kOutput, calls=%fused_computation.27 | convolution fusion | flops 2522087424 | bytes 18110468 | tf_op jit(solution)/shard_map/cond/branch_1_fun/dot_general | solution.py:102
  86.9 6.2 broadcast_in_dim.396
  113.2 78.5 %conditional.7 = (bf16[512,768]{1,0:T(8,128)(2,1)}, bf16[2,512,768]{2,1,0:T(8,128)(2,1)}, f32[2,512,768]{2,1,0:T(8,128)}, f32[2,512,1]{1,2,0:T(1,128)}, bf16[2,5...) conditional(s32[]{:T(128)} %convert_element_type.807, ...), branch_computations={%region_6.7_spmd, %region_7.12_spmd} | conditional | flops 8220219392 | bytes 168822080 | solution.py:325
  116.7 6.3 convolution_add_fusion.1
  123.1 6.1 copy.91
  135.8 3.5 fusion.47
  143.9 5.7 fusion.72
  155.6 19.4 %bitcast_dynamic-update-slice_fusion.8 = (bf16[2,512,3072]{2,1,0:T(8,128)(2,1)}, bf16[512,3072]{1,0:T(8,128)(2,1)S(1)}, f32[512,3072]{1,0:T(8,128)S(1)}) fusion(bf16[2,512,3072]{2,1,0:T(8,128)(2,1)} %get-tuple-element.1697, s32[]{:T(128)S(6)} %min.20, f32[3072]{0:T(1024)S(1)} %convert_element_type.710, bf16[768,3072]{1,0:T(8,128)(2,1)} %get-tuple-element.1682, ...), kind=kOutput, calls=%fused_computation.114 | convolution fusion | flops 2522087424 | bytes 18110468 | tf_op jit(solution)/shard_map/cond/branch_1_fun/dot_general | solution.py:102
  175.1 5.1 fusion.368
  182.4 3.3 bitcast_dynamic-update-slice_fusion.7
  196.1 4.4 conditional.8
  202.3 19.2 %conditional.9 = (bf16[512,768]{1,0:T(8,128)(2,1)}, f32[768]{0:T(1024)S(1)}, f32[768]{0:T(1024)S(1)}, f32[768,2304]{1,0:T(8,128)}, f32[2304]{0:T(1024)S(1)}, /*i...) conditional(s32[]{:T(128)} %convert_element_type.811, ...), branch_computations={%region_18.19_spmd, %region_19.30_spmd} | conditional | flops 16692826112 | bytes 289874976 | solution.py:359
  202.3 4.7 broadcast_in_dim.419
  207.1 4.2 broadcast_in_dim.421
  211.3 3.4 broadcast_in_dim.416
  222.8 150.9 %collective-permute-done.2 = bf16[512,768]{1,0:T(8,128)(2,1)} collective-permute-done((bf16[512,768]{1,0:T(8,128)(2,1)}, bf16[512,768]{1,0:T(8,128)(2,1)}, u32[]{:S(2)}, u32[]{:S(2)}) %collective-permute-start.2) | collective-permute-done | bytes 786464 | tf_op jit(solution)/shard_map/ppermute | solution.py:19
  373.7 107.4 %conditional.10 = (bf16[512,768]{1,0:T(8,128)(2,1)}, f32[768]{0:T(1024)S(1)}, f32[768]{0:T(1024)S(1)}, f32[768,2304]{1,0:T(8,128)}, f32[2304]{0:T(1024)S(1)}, /*...) conditional(s32[]{:T(128)} %convert_element_type.810, ...), branch_computations={%region_30.31_spmd.clone, %region_31.42_spmd.clone} | conditional | flops 16699914240 | bytes 341140704 | solution.py:359
  388.1 8.1 multiply_reduce_fusion.2
  396.2 7.0 multiply_convert_fusion.2
  413.3 19.6 %convert_reduce_fusion.9 = (f32[3072]{0:T(1024)S(1)}, bf16[512,3072]{1,0:T(8,128)(2,1)S(1)}) fusion(f32[2,512,3072]{2,1,0:T(8,128)} %get-tuple-element.2080, s32[]{:T(128)S(6)} %min.25, bf16[512,768]{1,0:T(8,128)(2,1)S(1)} %copy-done.28, bf16[3072,768]{1,0:T(8,128)(2,1)S(1)} %bitcast.727), kind=kOutput, calls=%fused_computation.499 | convolution fusion | flops 2532307968 | bytes 14954500 | tf_op jit(solution)/shard_map/cond/branch_1_fun/rd,fd->rf/dot_general | solution.py:154
  433.0 5.8 fusion.313
  442.7 8.2 convolution_add_fusion.7
  452.3 11.1 %convolution_add_fusion.9 = f32[768,3072]{1,0:T(8,128)} fusion(f32[768,3072]{1,0:T(8,128)} %get-tuple-element.2095, bf16[512,3072]{1,0:T(8,128)(2,1)} %copy-done.39, bf16[2,512,768]{2,1,0:T(8,128)(2,1)} %get-tuple-element.2096, s32[]{:T(128)S(6)} %min.25), kind=kOutput, calls=%fused_computation.519 | convolution fusion | flops 2418278400 | bytes 22806532 | tf_op jit(solution)/shard_map/cond/branch_1_fun/rd,rf->df/dot_general | solution.py:157
  463.4 11.0 %convolution_add_fusion.8 = f32[3072,768]{1,0:T(8,128)} fusion(f32[3072,768]{1,0:T(8,128)} %get-tuple-element.2098, bf16[512,768]{1,0:T(8,128)(2,1)S(1)} %copy-done.28, bf16[2,512,3072]{2,1,0:T(8,128)(2,1)} %get-tuple-element.2099, s32[]{:T(128)S(6)} %min.25), kind=kOutput, calls=%fused_computation.518 | convolution fusion | flops 2418278400 | bytes 22806532 | tf_op jit(solution)/shard_map/cond/branch_1_fun/rf,rd->fd/dot_general | solution.py:152
  485.7 106.4 %conditional.11 = (f32[768]{0:T(1024)S(1)}, f32[768]{0:T(1024)S(1)}, f32[768,2304]{1,0:T(8,128)}, f32[2304]{0:T(1024)S(1)}, f32[768,768]{1,0:T(8,128)}, /*index=...) conditional(s32[]{:T(128)} %convert_element_type.809, ...), branch_computations={%region_42.43_spmd, %region_43.54_spmd} | conditional | flops 16699914240 | bytes 340360416 | solution.py:359
  500.1 7.9 multiply_reduce_fusion.1
  508.1 7.0 multiply_convert_fusion.1
  525.2 19.3 %convert_reduce_fusion.6 = (f32[3072]{0:T(1024)S(1)}, bf16[512,3072]{1,0:T(8,128)(2,1)S(1)}) fusion(f32[2,512,3072]{2,1,0:T(8,128)} %get-tuple-element.1854, s32[]{:T(128)S(6)} %min.24, bf16[512,768]{1,0:T(8,128)(2,1)S(1)} %copy-done.26, bf16[3072,768]{1,0:T(8,128)(2,1)S(1)} %bitcast.729), kind=kOutput, calls=%fused_computation.390 | convolution fusion | flops 2532307968 | bytes 14954500 | tf_op jit(solution)/shard_map/cond/branch_1_fun/rd,fd->rf/dot_general | solution.py:154
  544.6 5.8 fusion.243
  554.0 8.2 convolution_add_fusion.3
  563.6 11.1 %convolution_add_fusion.5 = f32[768,3072]{1,0:T(8,128)} fusion(f32[768,3072]{1,0:T(8,128)} %get-tuple-element.1858, bf16[512,3072]{1,0:T(8,128)(2,1)} %copy-done.40, bf16[2,512,768]{2,1,0:T(8,128)(2,1)} %get-tuple-element.1859, s32[]{:T(128)S(6)} %min.24), kind=kOutput, calls=%fused_computation.410 | convolution fusion | flops 2418278400 | bytes 22806532 | tf_op jit(solution)/shard_map/cond/branch_1_fun/rd,rf->df/dot_general | solution.py:157
  574.7 11.0 %convolution_add_fusion.4 = f32[3072,768]{1,0:T(8,128)} fusion(f32[3072,768]{1,0:T(8,128)} %get-tuple-element.1861, bf16[512,768]{1,0:T(8,128)(2,1)S(1)} %copy-done.26, bf16[2,512,3072]{2,1,0:T(8,128)(2,1)} %get-tuple-element.1862, s32[]{:T(128)S(6)} %min.24), kind=kOutput, calls=%fused_computation.409 | convolution fusion | flops 2418278400 | bytes 22806532 | tf_op jit(solution)/shard_map/cond/branch_1_fun/rf,rd->fd/dot_general | solution.py:152
  595.0 5.2 convert_element_type.816
  600.3 6.4 convert_element_type.832
  606.8 6.6 convert_element_type.828
  613.5 13.5 %reduce-scatter.7.cloned.1.call-done = bf16[192,768]{1,0:T(8,128)(2,1)} async-done(((bf16[768,768]{1,0:T(8,128)(2,1)}), bf16[192,768]{1,0:T(8,128)(2,1)}) %reduce-scatter.7.cloned.1.call-update) | async-done | bytes 294928 | tf_op jit(solution)/shard_map/reduce_scatter | solution.py:391
  627.0 67.4 %reduce-scatter.5.cloned.1.call-done = bf16[192,2304]{1,0:T(8,128)(2,1)} async-done(((bf16[768,2304]{1,0:T(8,128)(2,1)}), bf16[192,2304]{1,0:T(8,128)(2,1)}) %reduce-scatter.5.cloned.1.call-update) | async-done | bytes 884752 | tf_op jit(solution)/shard_map/reduce_scatter | solution.py:385
  694.4 87.9 %reduce-scatter.11.cloned.1.call-done = bf16[768,768]{1,0:T(8,128)(2,1)} async-done(((bf16[3072,768]{1,0:T(8,128)(2,1)}), bf16[768,768]{1,0:T(8,128)(2,1)}) %reduce-scatter.11.cloned.1.call-update) | async-done | bytes 1179664 | tf_op jit(solution)/shard_map/reduce_scatter | solution.py:409
  782.3 88.0 %reduce-scatter.9.cloned.1.call-done = bf16[192,3072]{1,0:T(8,128)(2,1)} async-done(((bf16[768,3072]{1,0:T(8,128)(2,1)}), bf16[192,3072]{1,0:T(8,128)(2,1)}) %reduce-scatter.9.cloned.1.call-update) | async-done | bytes 1179664 | tf_op jit(solution)/shard_map/reduce_scatter | solution.py:403
  874.3 18.2 %all-reduce.10 = (bf16[768]{0:T(1024)(128)(2,1)S(1)}, bf16[768]{0:T(1024)(128)(2,1)S(1)}, bf16[2304]{0:T(1024)(128)(2,1)S(1)}, bf16[768]{0:T(1024)(128)(2,1)S(1)...) all-reduce(bf16[768]{0:T(1024)(128)(2,1)S(1)} %convert_element_type, ...), channel_id=2, replica_groups=mesh['section'=2,'dp'=4,'replica'=4] {'dp'}, use_global_device_ids=true, to_apply=%region_54.55.clone | all-reduce | flops 9984 | bytes 39936
  893.1 10.5 %all-reduce.8 = (bf16[192]{0:T(256)(128)(2,1)S(1)}, bf16[192]{0:T(256)(128)(2,1)S(1)}, bf16[576]{0:T(1024)(128)(2,1)S(1)}, bf16[192]{0:T(256)(128)(2,1)S(1)}, bf...) all-reduce(bf16[192]{0:T(256)(128)(2,1)S(1)} %dynamic-slice.1, ...), channel_id=1, replica_groups=mesh['section'=2,'dp'=4,'replica'=4] {'replica'}, use_global_device_ids=true, to_apply=%region_55.56 | all-reduce | flops 2496 | bytes 9984 | tf_op jit(solution)/shard_map/psum | solution.py:417
  906.5 62.4 %all-reduce.13.cloned.1.call-done = (bf16[192,2304]{1,0:T(8,128)(2,1)}, bf16[192,768]{1,0:T(8,128)(2,1)}, bf16[192,3072]{1,0:T(8,128)(2,1)}, bf16[768,768]{1,0:T(8,128)(2,1)}) async-done(((bf16[192,2304]{1,0:T(8,128)(2,1)}, bf16[192,768]{1,0:T(8,128)(2,1)}, bf16[192,3072]{1,0:T(8,128)(2,1)}, bf16[768,768]{1,0:T(8,128)(2,1)}), (bf16[192,2304]{1,0:T(8,128)(2,1)}, bf16[192,768]{1,0:T(8,128)(2,1)}, ...) | async-done | bytes 3538960 | tf_op jit(solution)/shard_map/psum | solution.py:419
  (436 shorter events, 186.2 us)
Async XLA Ops:
  7.2 619.8 %reduce-scatter.7.cloned.1.call-start = ((), (), s32[]{:S(2)}) async-start(), calls=%async_computation.5 | async-start | bytes 1474560 | tf_op jit(solution)/shard_map/reduce_scatter | solution.py:391
  46.5 6.8 copy-start.10
  46.9 6.4 copy-start.5
  53.3 8.4 copy-start.19
  53.3 8.4 copy-start.82
  53.3 8.4 copy-start.85
  58.3 22.5 %slice-start.8 = ((s8[4718592]{0:T(1024)(128)(4,1)}), s8[524288]{0:T(1024)(128)(4,1)S(1)}, s32[]{:S(2)}) async-start(s8[4718592]{0:T(1024)(128)(4,1)} %bitcast.722), calls=%async_computation.17 | async-start | bytes 1048576 | tf_op jit(solution)/shard_map/cond
  61.7 19.1 %slice-start.9 = ((s8[4718592]{0:T(1024)(128)(4,1)}), s8[4194304]{0:T(1024)(128)(4,1)S(1)}, s32[]{:S(2)}) async-start(s8[4718592]{0:T(1024)(128)(4,1)} %bitcast.722), calls=%async_computation.18 | async-start | bytes 8388608 | tf_op jit(solution)/shard_map/cond
  93.0 8.2 copy-start.20
  93.0 8.2 copy-start.83
  93.0 8.2 copy-start.86
  96.3 7.5 copy-start.101
  96.3 7.5 copy-start.103
  100.0 9.5 copy-start.6
  100.0 9.5 copy-start.11
  109.7 3.5 collective-permute-start
  175.1 5.2 copy-start.88
  175.1 5.2 copy-start.92
  175.1 5.2 copy-start.22
  175.1 5.2 copy-start.59
  175.1 5.2 copy-start.112
  191.8 4.4 collective-permute-start.1
  221.5 152.2 %copy-start = (f32[768,768]{1,0:T(8,128)}, f32[768,768]{1,0:T(8,128)S(1)}, u32[]{:S(2)}) copy-start(f32[768,768]{1,0:T(8,128)S(1)} %get-tuple-element.2002) | copy-start | bytes 7077892
  221.5 152.2 %copy-start.70 = (f32[768]{0:T(1024)}, f32[768]{0:T(1024)S(1)}, u32[]{:S(2)}) copy-start(f32[768]{0:T(1024)S(1)} %get-tuple-element.2003) | copy-start | bytes 9220
  221.5 152.2 %collective-permute-start.2 = (bf16[512,768]{1,0:T(8,128)(2,1)}, bf16[512,768]{1,0:T(8,128)(2,1)}, u32[]{:S(2)}, u32[]{:S(2)}) collective-permute-start(bf16[512,768]{1,0:T(8,128)(2,1)} %get-tuple-element.2010), channel_id=1, source_target_pairs={{16,0},{17,1},{18,2},{19,3},{20,4},{21,5},{22,6},{23,7},{24,8},{25... | collective-permute-start | bytes 2359304 | tf_op jit(solution)/shard_map/ppermute | solution.py:19
  373.8 10.9 %copy-start.8 = (bf16[2,512,12,64]{1,3,2,0:T(8,128)(2,1)S(1)}, bf16[2,512,12,64]{1,3,2,0:T(8,128)(2,1)}, u32[]{:S(2)}) copy-start(bf16[2,512,12,64]{1,3,2,0:T(8,128)(2,1)} %get-tuple-element.2071) | copy-start | bytes 4718596 | tf_op jit(solution)/shard_map/cond
  373.8 10.9 %copy-start.13 = (bf16[2,512,12,64]{1,3,2,0:T(8,128)(2,1)S(1)}, bf16[2,512,12,64]{1,3,2,0:T(8,128)(2,1)}, u32[]{:S(2)}) copy-start(bf16[2,512,12,64]{1,3,2,0:T(8,128)(2,1)} %get-tuple-element.2072) | copy-start | bytes 4718596 | tf_op jit(solution)/shard_map/cond
  411.1 21.8 %slice-start.4 = ((s8[4718592]{0:T(1024)(128)(4,1)}), s8[4194304]{0:T(1024)(128)(4,1)S(1)}, s32[]{:S(2)}) async-start(s8[4718592]{0:T(1024)(128)(4,1)} %bitcast.712), calls=%async_computation.13 | async-start | bytes 8388608 | tf_op jit(solution)/shard_map/cond
  413.3 19.6 %slice-start.5 = ((s8[4718592]{0:T(1024)(128)(4,1)}), s8[524288]{0:T(1024)(128)(4,1)S(1)}, s32[]{:S(2)}) async-start(s8[4718592]{0:T(1024)(128)(4,1)} %bitcast.712), calls=%async_computation.14 | async-start | bytes 1048576 | tf_op jit(solution)/shard_map/cond
  432.9 5.8 copy-start.39
  463.4 13.7 %copy-start.1 = (f32[768,768]{1,0:T(8,128)S(1)}, f32[768,768]{1,0:T(8,128)}, u32[]{:S(2)}) copy-start(f32[768,768]{1,0:T(8,128)} %get-tuple-element.2090) | copy-start | bytes 7077892 | tf_op jit(solution)/shard_map/cond
  474.5 4.7 copy-start.98
  481.1 4.5 collective-permute-start.3
  485.8 10.9 %copy-start.9 = (bf16[2,512,12,64]{1,3,2,0:T(8,128)(2,1)S(1)}, bf16[2,512,12,64]{1,3,2,0:T(8,128)(2,1)}, u32[]{:S(2)}) copy-start(bf16[2,512,12,64]{1,3,2,0:T(8,128)(2,1)} %get-tuple-element.1830) | copy-start | bytes 4718596 | tf_op jit(solution)/shard_map/cond
  485.8 10.9 %copy-start.14 = (bf16[2,512,12,64]{1,3,2,0:T(8,128)(2,1)S(1)}, bf16[2,512,12,64]{1,3,2,0:T(8,128)(2,1)}, u32[]{:S(2)}) copy-start(bf16[2,512,12,64]{1,3,2,0:T(8,128)(2,1)} %get-tuple-element.1833) | copy-start | bytes 4718596 | tf_op jit(solution)/shard_map/cond
  523.0 21.6 %slice-start.6 = ((s8[4718592]{0:T(1024)(128)(4,1)}), s8[4194304]{0:T(1024)(128)(4,1)S(1)}, s32[]{:S(2)}) async-start(s8[4718592]{0:T(1024)(128)(4,1)} %bitcast.714), calls=%async_computation.15 | async-start | bytes 8388608 | tf_op jit(solution)/shard_map/cond
  525.2 19.4 %slice-start.7 = ((s8[4718592]{0:T(1024)(128)(4,1)}), s8[524288]{0:T(1024)(128)(4,1)S(1)}, s32[]{:S(2)}) async-start(s8[4718592]{0:T(1024)(128)(4,1)} %bitcast.714), calls=%async_computation.16 | async-start | bytes 1048576 | tf_op jit(solution)/shard_map/cond
  544.5 5.8 copy-start.40
  574.7 13.7 %copy-start.3 = (f32[768,768]{1,0:T(8,128)S(1)}, f32[768,768]{1,0:T(8,128)}, u32[]{:S(2)}) copy-start(f32[768,768]{1,0:T(8,128)} %get-tuple-element.1850) | copy-start | bytes 7077892 | tf_op jit(solution)/shard_map/cond
  585.8 4.7 copy-start.99
  594.9 99.4 %reduce-scatter.5.cloned.1.call-start = ((), (), s32[]{:S(2)}) async-start(), calls=%async_computation.4 | async-start | bytes 4423680 | tf_op jit(solution)/shard_map/reduce_scatter | solution.py:385
  600.3 182.0 %reduce-scatter.11.cloned.1.call-start = ((), (), s32[]{:S(2)}) async-start(), calls=%async_computation.7 | async-start | bytes 5898240 | tf_op jit(solution)/shard_map/reduce_scatter | solution.py:409
  606.7 263.5 %reduce-scatter.9.cloned.1.call-start = ((), (), s32[]{:S(2)}) async-start(), calls=%async_computation.6 | async-start | bytes 5898240 | tf_op jit(solution)/shard_map/reduce_scatter | solution.py:403
  613.4 256.9 %copy-start.117 = (u32[32]{0:T(128)S(1)}, u32[32]{0:T(128)}, u32[]{:S(2)}) copy-start(u32[32]{0:T(128)} %constant.1355) | copy-start | bytes 388
  613.4 259.5 %copy-start.75 = (f32[768]{0:T(1024)S(1)}, f32[768]{0:T(1024)}, u32[]{:S(2)}) copy-start(f32[768]{0:T(1024)} %get-tuple-element.2031) | copy-start | bytes 9220
  613.4 355.4 %all-reduce.13.cloned.1.call-start = ((), (), s32[]{:S(2)}) async-start(), calls=%async_computation.8 | async-start | bytes 7077888 | tf_op jit(solution)/shard_map/psum | solution.py:419
  968.8 5.9 copy-start.57
  968.8 7.2 copy-start.69
  (64 other events, 145.5 us)
Sparse Core Ops, SparseCore 0:
  595.1 31.8 reduce-scatter.6
  629.3 65.0 reduce-scatter.4
  696.7 85.5 reduce-scatter.10
  784.4 85.7 reduce-scatter.8
  873.5 95.2 all-reduce.12
where the time goes:
time: 991 us; the launch traced here: 984 us
  waiting for transfers between devices  476 us (48%)
  matrix products  237 us (24%)
  other arithmetic  110 us (11%)
  local copies, waits for them, and re-layouts  98.2 us (10%)
  blocking collectives  28.7 us (3%)
  between operations  16.2 us (2%)
    ppermute x4, waiting for transfers between devices, shifted_2(): return lax.ppermute(value, axis, pairs)  157 us
    reduce_scatter x1, waiting for transfers between devices, body(): lax.psum_scatter(sum_up_weight.astype(jnp.bfloat16), 'dp', scatter_dimens...  88 us
    reduce_scatter x1, waiting for transfers between devices, body(): lax.psum_scatter(sum_down_weight.astype(jnp.bfloat16), 'dp', scatter_dime...  87.9 us
    reduce_scatter x1, waiting for transfers between devices, body(): lax.psum_scatter(sum_qkv_weight.astype(jnp.bfloat16), 'dp', scatter_dimen...  67.4 us
    psum x1, waiting for transfers between devices, body(): lax.psum(shares[2].astype(jnp.bfloat16), 'replica').astype(jnp.float32)  62.4 us
    dot_general x2, matrix products, layer_backward(): jnp.einsum('rd,fd->rf', grad_out, down_weight, preferred_element_type=jnp...  38.9 us
    dot_general x2, matrix products, layer_forward(): jnp.dot(mlp_in, up_weight, preferred_element_type=jnp.float32) + up_bias  38.5 us
    dot_general x2, matrix products, layer_backward(): jnp.einsum('rd,rf->df', mlp_in, grad_up_pre, preferred_element_type=jnp.f...  22.2 us
  transfers between devices with their start and end apart: 9, of which 9 were waited for; matrix products, arithmetic and copies ran while one was open for 2% of the time, Pallas kernels for 0%

commit v1 on v0

v1 whole, which is shorter than its diff:
```python
import functools

import jax
import jax.numpy as jnp
from jax import lax
from jax.experimental import pallas as pl
from jax.experimental.pallas import tpu as pltpu
from jax.sharding import PartitionSpec as P

HEADS = 12
HEAD_DIM = 64
ROTARY = 16
HALF = ROTARY // 2
EPSILON = 1e-05
ROTARY_BASE = 10000.0
MASKED = -1e30
SCALE = HEAD_DIM**-0.5
F32 = jnp.float32
BF16 = jnp.bfloat16
ANY = pl.BlockSpec(memory_space=pl.ANY)
VMEM = pl.BlockSpec(memory_space=pltpu.VMEM)
SMEM = pl.BlockSpec(memory_space=pltpu.SMEM)
ROW_CHUNK = 128
QKV_TILE = 256
FF_TILE = 512


def dims_dot(left, right, left_dim, right_dim):
    return lax.dot_general(
        left, right, (((left_dim,), (right_dim,)), ((), ())), preferred_element_type=F32
    )


def normal_parts(v):
    t = 1.0 / (1.0 + (0.3275911 * 0.7071067811865476) * jnp.abs(v))
    bell = jnp.exp(-0.5 * v * v)
    series = 0.7107068705 + t * (-0.7265760135 + t * 0.5307027145)
    tail = t * (0.127414796 + t * (-0.142248368 + t * series)) * bell
    return jnp.where(v >= 0, 1.0 - tail, tail), bell * 0.3989422804014327


class Copies:
    def __init__(self, sems):
        self.sems, self.copies = sems, []

    def start(self, src, dst):
        copy = pltpu.make_async_copy(src, dst, self.sems.at[len(self.copies)])
        copy.start()
        self.copies.append(copy)
        return copy

    def wait(self):
        for copy in self.copies:
            copy.wait()


def forward_kernel(moment, micros, n_alias, *refs):
    (
        lengths, tokens_h, received_h, attn_gain, attn_shift, qkv_bias, out_bias, mlp_gain, mlp_shift,
        up_bias, down_bias, cosine, sine, qkv_h, out_h, up_h, down_h,
    ) = refs[:17]
    (
        y_send_h, y_h, attn_in_h, mlp_in_h, queries_h, keys_h, values_h, probs_h, context_h, hidden_h, slope_h,
        qkv_w, out_w, up_w, down_w, x, attn_in, mlp_in, attn_in_t, mlp_in_t, heads_t, context_t, hidden_t, slope,
        bias, total, probs, y, in_sems, out_sems, probs_sems,
    ) = refs[17 + n_alias :]
    section = lax.axis_index("section")
    micro = moment - section
    rows, width = x.shape
    hidden_width = up_w.shape[1]
    half = rows // 2

    @pl.when((micro >= 0) & (micro < micros))
    def _():
        loads = [
            pltpu.make_async_copy(src, dst, in_sems.at[i])
            for i, (src, dst) in enumerate(((qkv_h, qkv_w), (out_h, out_w), (up_h, up_w), (down_h, down_w)))
        ]
        own = pltpu.make_async_copy(tokens_h.at[micro], x, in_sems.at[4])
        passed = pltpu.make_async_copy(received_h, x, in_sems.at[4])

        @pl.when(section == 0)
        def _():
            own.start()

        @pl.when(section != 0)
        def _():
            passed.start()

        loads[0].start()
        stores = Copies(out_sems)
        length = lengths[micro]
        key_ids = lax.broadcasted_iota(jnp.int32, (rows, rows), 0)
        query_ids = lax.broadcasted_iota(jnp.int32, (rows, rows), 1)
        bias[...] = jnp.where((key_ids <= query_ids) & (key_ids < length), 0.0, MASKED)
        probs[:, half:, :half] = jnp.zeros((probs.shape[0], half, half), BF16)
        own.wait()

        for start in range(0, rows, ROW_CHUNK):
            part = slice(start, start + ROW_CHUNK)
            block = x[part, :].astype(F32)
            centred = block - jnp.mean(block, axis=-1, keepdims=True)
            unit = centred * lax.rsqrt(jnp.mean(centred * centred, axis=-1, keepdims=True) + EPSILON)
            attn = (unit * attn_gain[...].astype(F32) + attn_shift[...].astype(F32)).astype(BF16)
            mlp = (unit * mlp_gain[...].astype(F32) + mlp_shift[...].astype(F32)).astype(BF16)
            attn_in[part, :] = attn
            mlp_in[part, :] = mlp
            attn_in_t[:, part] = attn.T
            mlp_in_t[:, part] = mlp.T
        loads[0].wait()
        for load in loads[1:]:
            load.start()
        stores.start(attn_in_t, attn_in_h.at[micro])
        stores.start(mlp_in_t, mlp_in_h.at[micro])

        cos_rows, sin_rows = cosine[...], sine[...]
        for start in range(0, 3 * width, QKV_TILE):
            part = slice(start, start + QKV_TILE)
            projected = jnp.dot(attn_in[...], qkv_w[:, part], preferred_element_type=F32)
            turned = (projected + qkv_bias[:, part].astype(F32)).T
            if start >= 2 * width:
                heads_t[part, :] = turned.astype(BF16)
                continue
            for at in range(0, QKV_TILE, HEAD_DIM):
                low, high = turned[at : at + HALF], turned[at + HALF : at + ROTARY]
                heads_t[start + at : start + at + HEAD_DIM, :] = jnp.concatenate(
                    [
                        low * cos_rows - high * sin_rows,
                        high * cos_rows + low * sin_rows,
                        turned[at + ROTARY : at + HEAD_DIM],
                    ],
                    axis=0,
                ).astype(BF16)
        stores.start(heads_t.at[0:width], queries_h.at[micro])
        stores.start(heads_t.at[width : 2 * width], keys_h.at[micro])
        stores.start(heads_t.at[2 * width :], values_h.at[micro])

        def softmax(scores):
            raised = jnp.exp(scores - jnp.max(scores, axis=0, keepdims=True))
            return (raised * (1.0 / jnp.sum(raised, axis=0, keepdims=True))).astype(BF16)

        def attend(head, slot):
            at = pl.multiple_of(head * HEAD_DIM, HEAD_DIM)
            query = heads_t[pl.ds(at, HEAD_DIM), :] * jnp.bfloat16(SCALE)
            key = heads_t[pl.ds(width + at, HEAD_DIM), :]
            value = heads_t[pl.ds(2 * width + at, HEAD_DIM), :]
            early = softmax(dims_dot(key[:, :half], query[:, :half], 0, 0) + bias[:half, :half])
            late = softmax(dims_dot(key, query[:, half:], 0, 0) + bias[:, half:])
            probs[slot, :half, :half] = early
            probs[slot, :, half:] = late
            place = pl.ds(at, HEAD_DIM)
            context_t[place, :half] = jnp.dot(value[:, :half], early, preferred_element_type=F32).astype(BF16)
            context_t[place, half:] = jnp.dot(value, late, preferred_element_type=F32).astype(BF16)

        def probs_copy(head, slot):
            return pltpu.make_async_copy(probs.at[slot], probs_h.at[micro, head], probs_sems.at[slot])

        def attend_pair(pair, carry):
            first_slot = 2 * lax.rem(pair, 2)

            @pl.when(pair >= 2)
            def _():
                for own_head in range(2):
                    probs_copy(2 * pair + own_head - 4, first_slot + own_head).wait()

            for own_head in range(2):
                attend(2 * pair + own_head, first_slot + own_head)
            for own_head in range(2):
                probs_copy(2 * pair + own_head, first_slot + own_head).start()
            return carry

        lax.fori_loop(0, HEADS // 2, attend_pair, 0)
        for head in range(HEADS - 4, HEADS):
            probs_copy(head, head % 4).wait()
        stores.start(context_t, context_h.at[micro])

        for load in loads[1:]:
            load.wait()
        total[...] = (
            dims_dot(context_t[...], out_w[...], 0, 0)
            + x[...].astype(F32)
            + (out_bias[...].astype(F32) + down_bias[...].astype(F32))
        )
        for start in range(0, hidden_width, FF_TILE):
            part = slice(start, start + FF_TILE)
            up = jnp.dot(mlp_in[...], up_w[:, part], preferred_element_type=F32)
            up = up + up_bias[:, part].astype(F32)
            share, density = normal_parts(up)
            hidden = (up * share).astype(BF16)
            slope[:, part] = (share + up * density).astype(BF16)
            hidden_t[part, :] = hidden.T
            stores.start(hidden_t.at[part], hidden_h.at[micro, part])
            stores.start(slope.at[:, part], slope_h.at[micro, :, part])
            total[...] += jnp.dot(hidden, down_w[part, :], preferred_element_type=F32)
        y[...] = total[...].astype(BF16)
        stores.start(y, y_send_h)
        stores.start(y, y_h.at[micro])
        stores.wait()


def forward_call(moment, lengths, tokens, received, weights, tables, stash):
    (
        attn_gain, attn_shift, qkv_weight, qkv_bias, out_weight, out_bias, mlp_gain, mlp_shift, up_weight, up_bias,
        down_weight, down_bias,
    ) = weights
    micros, rows, width = tokens.shape
    hidden_width = up_weight.shape[1]
    wide, tall = (micros, rows, width), (micros, width, rows)
    shapes = [
        (rows, width), wide, tall, tall, tall, tall, tall, (micros, HEADS, rows, rows), tall,
        (micros, hidden_width, rows), (micros, rows, hidden_width),
    ]
    kept = () if stash is None else tuple(stash)
    buffers = [
        qkv_weight.shape, out_weight.shape, up_weight.shape, down_weight.shape, (rows, width), (rows, width),
        (rows, width), (width, rows), (width, rows), (3 * width, rows), (width, rows), (hidden_width, rows),
        (rows, hidden_width),
    ]
    outs = pl.pallas_call(
        functools.partial(forward_kernel, moment, micros, len(kept)),
        out_shape=[jax.ShapeDtypeStruct(shape, BF16) for shape in shapes],
        in_specs=[SMEM, ANY, ANY] + [VMEM] * 10 + [ANY] * (4 + len(kept)),
        out_specs=[ANY] * len(shapes),
        scratch_shapes=[pltpu.VMEM(shape, BF16) for shape in buffers]
        + [
            pltpu.VMEM((rows, rows), F32),
            pltpu.VMEM((rows, width), F32),
            pltpu.VMEM((4, rows, rows), BF16),
            pltpu.VMEM((rows, width), BF16),
            pltpu.SemaphoreType.DMA((5,)),
            pltpu.SemaphoreType.DMA((8 + 2 * (hidden_width // FF_TILE),)),
            pltpu.SemaphoreType.DMA((4,)),
        ],
        input_output_aliases={17 + i: 1 + i for i in range(len(kept))},
        compiler_params=pltpu.CompilerParams(vmem_limit_bytes=56 << 20),
        cost_estimate=pl.CostEstimate(
            flops=2 * rows * width * (4 * width + 2 * hidden_width) + 4 * rows * rows * width,
            bytes_accessed=40 << 20,
            transcendentals=rows * hidden_width,
        ),
        name="layer_forward",
    )(
        lengths, tokens, received, attn_gain, attn_shift, qkv_bias, out_bias, mlp_gain, mlp_shift, up_bias,
        down_bias, *tables, qkv_weight, out_weight, up_weight, down_weight, *kept,
    )
    return outs[0], outs[1:]


def backward_kernel(moment, micros, n_alias, *refs):
    n_in = 17 + micros
    lengths, cotangent_h, received_h, tokens_h = refs[:4]
    passed_h = refs[4 : 4 + micros]
    (
        attn_gain, mlp_gain, cosine, sine, qkv_h, out_h, up_h, down_h, queries_h, keys_h, values_h, probs_h,
        context_h, slope_h,
    ) = refs[4 + micros : 18 + micros]
    (
        send_h, grad_in_h, grad_heads_h, grad_up_h, grad_out_h, vectors_h,
        qkv_w, out_w, up_w, down_w, queries, keys, values, context, slope, probs, grad_out, x, grad_context,
        grad_up, grad_heads, grad_low, grad_mlp, grad_in, column_sums, vectors, in_sems, out_sems, probs_sems,
    ) = refs[18 + micros + n_alias :]
    section = lax.axis_index("section")
    last = lax.axis_size("section") - 1
    micro = moment - (last - section)
    rows, width = x.shape
    hidden_width = up_w.shape[1]
    half = rows // 2

    @pl.when((micro >= 0) & (micro < micros))
    def _():
        loads = [
            pltpu.make_async_copy(src, dst, in_sems.at[i])
            for i, (src, dst) in enumerate(
                (
                    (out_h, out_w), (down_h, down_w), (slope_h.at[micro], slope), (up_h, up_w),
                    (values_h.at[micro], values), (context_h.at[micro], context), (queries_h.at[micro], queries),
                    (keys_h.at[micro], keys), (qkv_h, qkv_w),
                )
            )
        ]
        own = pltpu.make_async_copy(cotangent_h.at[micro], grad_out, in_sems.at[9])
        passed = pltpu.make_async_copy(received_h, grad_out, in_sems.at[9])
        block = pltpu.make_async_copy(tokens_h.at[micro], x, in_sems.at[10])

        @pl.when(section == last)
        def _():
            own.start()

        @pl.when(section != last)
        def _():
            passed.start()

        for load in loads[:4]:
            load.start()

        @pl.when(section == 0)
        def _():
            block.start()

        for one, source in enumerate(passed_h):

            @pl.when((section != 0) & (micro == one))
            def _():
                pltpu.make_async_copy(source, x, in_sems.at[10]).start()

        stores = Copies(out_sems)
        length = lengths[micro]
        row_ids = lax.broadcasted_iota(jnp.int32, (rows, 1), 0)
        own.wait()
        grad_wide = jnp.where(row_ids < length, grad_out[...].astype(F32), 0.0)
        grad_out[...] = grad_wide.astype(BF16)
        vectors[...] = jnp.zeros_like(vectors)
        vectors[7:8, :] = jnp.sum(grad_wide, axis=0, keepdims=True)
        stores.start(grad_out, grad_out_h.at[micro])
        loads[0].wait()
        for load in loads[4:]:
            load.start()
        grad_context[...] = dims_dot(out_w[...], grad_out[...], 1, 1).astype(BF16)

        for load in loads[1:4]:
            load.wait()
        for start in range(0, hidden_width, FF_TILE):
            part = slice(start, start + FF_TILE)
            grad_hidden = dims_dot(grad_out[...], down_w[part, :], 1, 1)
            grad_pre = (grad_hidden * slope[:, part].astype(F32)).astype(BF16)
            grad_up[:, part] = grad_pre
            stores.start(grad_up.at[:, part], grad_up_h.at[micro, :, part])
            sums = jnp.sum(grad_pre.astype(F32), axis=0, keepdims=True)
            for at in range(0, FF_TILE, 128):
                row, column = divmod(start + at, width)
                vectors[8 + row : 9 + row, column : column + 128] = sums[:, at : at + 128]
            back = dims_dot(up_w[:, part], grad_pre, 1, 1)
            if start == 0:
                grad_mlp[...] = back
            else:
                grad_mlp[...] += back

        for load in loads[4:8]:
            load.wait()
        cos_rows, sin_rows = cosine[...], sine[...]

        def turn_back(grad):
            low, high = grad[:HALF], grad[HALF:ROTARY]
            return jnp.concatenate(
                [low * cos_rows + high * sin_rows, high * cos_rows - low * sin_rows, grad[ROTARY:]], axis=0
            )

        def over_queries(left, early, late):
            both = dims_dot(left[:, half:], late, 1, 1)
            return jnp.concatenate([both[:, :half] + dims_dot(left[:, :half], early, 1, 1), both[:, half:]], axis=1)

        def attend(head, slot):
            at = pl.multiple_of(head * HEAD_DIM, HEAD_DIM)
            place = pl.ds(at, HEAD_DIM)
            query, key, value, grad = queries[place, :], keys[place, :], values[place, :], grad_context[place, :]
            inner = jnp.sum(grad.astype(F32) * context[place, :].astype(F32), axis=0, keepdims=True)
            early, late = probs[slot, :half, :half], probs[slot, :, half:]
            grad_early = dims_dot(value[:, :half], grad[:, :half], 0, 0) - inner[:, :half]
            grad_late = dims_dot(value, grad[:, half:], 0, 0) - inner[:, half:]
            grad_early = (early.astype(F32) * grad_early).astype(BF16)
            grad_late = (late.astype(F32) * grad_late).astype(BF16)
            grad_value = over_queries(grad, early, late)
            grad_key = over_queries(query, grad_early, grad_late)
            grad_query = jnp.concatenate(
                [
                    jnp.dot(key[:, :half], grad_early, preferred_element_type=F32),
                    jnp.dot(key, grad_late, preferred_element_type=F32),
                ],
                axis=1,
            )
            grad_heads[place, :] = turn_back(grad_query * SCALE).astype(BF16)
            grad_heads[pl.ds(width + at, HEAD_DIM), :] = turn_back(grad_key * SCALE).astype(BF16)
            grad_heads[pl.ds(2 * width + at, HEAD_DIM), :] = grad_value.astype(BF16)

        def probs_copy(head, slot):
            return pltpu.make_async_copy(probs_h.at[micro, head], probs.at[slot], probs_sems.at[slot])

        for head in range(2):
            probs_copy(head, head).start()

        def attend_pair(pair, carry):
            first_slot = 2 * lax.rem(pair, 2)

            @pl.when(pair < HEADS // 2 - 1)
            def _():
                for own_head in range(2):
                    probs_copy(2 * pair + 2 + own_head, 2 - first_slot + own_head).start()

            for own_head in range(2):
                probs_copy(2 * pair + own_head, first_slot + own_head).wait()
            for own_head in range(2):
                attend(2 * pair + own_head, first_slot + own_head)
            return carry

        lax.fori_loop(0, HEADS // 2, attend_pair, 0)
        stores.start(grad_heads, grad_heads_h.at[micro])

        loads[8].wait()
        block.wait()
        attn_column = jnp.broadcast_to(attn_gain[...].astype(F32), (8, width)).T[:, 0:1]
        mlp_column = jnp.broadcast_to(mlp_gain[...].astype(F32), (8, width)).T[:, 0:1]
        column_sums[...] = jnp.zeros_like(column_sums)

        def norm_chunk(index, carry):
            part = pl.ds(pl.multiple_of(index * ROW_CHUNK, ROW_CHUNK), ROW_CHUNK)
            grad_attn_in = jnp.dot(qkv_w[...], grad_heads[:, part], preferred_element_type=F32)
            grad_mlp_in = grad_mlp[:, part]
            turned = x[part, :].astype(F32).T
            centred = turned - jnp.mean(turned, axis=0, keepdims=True)
            inv_spread = lax.rsqrt(jnp.mean(centred * centred, axis=0, keepdims=True) + EPSILON)
            unit = centred * inv_spread
            grad_unit = grad_attn_in * attn_column + grad_mlp_in * mlp_column
            through = inv_spread * (
                grad_unit
                - jnp.mean(grad_unit, axis=0, keepdims=True)
                - unit * jnp.mean(grad_unit * unit, axis=0, keepdims=True)
            )
            exact = through.T + grad_out[part, :].astype(F32)
            low = exact.astype(BF16)
            grad_low[part, :] = low
            grad_in[part, :] = jnp.where(section == 0, exact, low.astype(F32))
            column_sums[0] += grad_attn_in * unit
            column_sums[1] += grad_attn_in
            column_sums[2] += grad_mlp_in * unit
            column_sums[3] += grad_mlp_in
            return carry

        lax.fori_loop(0, rows // ROW_CHUNK, norm_chunk, 0)
        stores.start(grad_low, send_h)
        stores.start(grad_in, grad_in_h.at[micro])
        columns = [jnp.sum(column_sums[i], axis=1, keepdims=True) for i in range(4)]
        for start in range(0, 3 * width, width):
            columns.append(jnp.sum(grad_heads[start : start + width, :].astype(F32), axis=1, keepdims=True))
        lanes = lax.broadcasted_iota(jnp.int32, (width, 128), 1)
        gathered = jnp.zeros((width, 128), F32)
        for lane, column in enumerate(columns):
            gathered = jnp.where(lanes == lane, column, gathered)
        vectors[0:7, :] = gathered.T[0:7, :]
        stores.start(vectors, vectors_h.at[micro])
        stores.wait()


def backward_call(moment, lengths, cotangent, received, tokens, passed, weights, tables, stash, kept):
    attn_gain, _, qkv_weight, _, out_weight, _, mlp_gain, _, up_weight, _, down_weight, _ = weights
    _, _, _, queries, keys, values, probs, context, _, slope = stash
    micros, rows, width = tokens.shape
    hidden_width = up_weight.shape[1]
    vector_rows = 16
    kept = () if kept is None else tuple(kept)
    outs = [
        jax.ShapeDtypeStruct((rows, width), BF16),
        jax.ShapeDtypeStruct((micros, rows, width), F32),
        jax.ShapeDtypeStruct((micros, 3 * width, rows), BF16),
        jax.ShapeDtypeStruct((micros, rows, hidden_width), BF16),
        jax.ShapeDtypeStruct((micros, rows, width), BF16),
        jax.ShapeDtypeStruct((micros, vector_rows, width), F32),
    ]
    tall = (width, rows)
    n_in = 18 + micros
    results = pl.pallas_call(
        functools.partial(backward_kernel, moment, micros, len(kept)),
        out_shape=outs,
        in_specs=[SMEM] + [ANY] * (3 + micros) + [VMEM] * 4 + [ANY] * (10 + len(kept)),
        out_specs=[ANY] * len(outs),
        scratch_shapes=[
            pltpu.VMEM(qkv_weight.shape, BF16),
            pltpu.VMEM(out_weight.shape, BF16),
            pltpu.VMEM(up_weight.shape, BF16),
            pltpu.VMEM(down_weight.shape, BF16),
            pltpu.VMEM(tall, BF16),
            pltpu.VMEM(tall, BF16),
            pltpu.VMEM(tall, BF16),
            pltpu.VMEM(tall, BF16),
            pltpu.VMEM((rows, hidden_width), BF16),
            pltpu.VMEM((4, rows, rows), BF16),
            pltpu.VMEM((rows, width), BF16),
            pltpu.VMEM((rows, width), BF16),
            pltpu.VMEM(tall, BF16),
            pltpu.VMEM((rows, hidden_width), BF16),
            pltpu.VMEM((3 * width, rows), BF16),
            pltpu.VMEM((rows, width), BF16),
            pltpu.VMEM(tall, F32),
            pltpu.VMEM((rows, width), F32),
            pltpu.VMEM((4, width, 128), F32),
            pltpu.VMEM((vector_rows, width), F32),
            pltpu.SemaphoreType.DMA((11,)),
            pltpu.SemaphoreType.DMA((5 + hidden_width // FF_TILE,)),
            pltpu.SemaphoreType.DMA((4,)),
        ],
        input_output_aliases={n_in + i: 1 + i for i in range(len(kept))},
        compiler_params=pltpu.CompilerParams(vmem_limit_bytes=58 << 20),
        cost_estimate=pl.CostEstimate(
            flops=2 * rows * width * (4 * width + 2 * hidden_width) + 8 * rows * rows * width,
            bytes_accessed=40 << 20,
            transcendentals=0,
        ),
        name="layer_backward",
    )(
        lengths, cotangent, received, tokens, *passed, attn_gain, mlp_gain, *tables, qkv_weight, out_weight,
        up_weight, down_weight, queries, keys, values, probs, context, slope, *kept,
    )
    return results[0], results[1:]


def shifted(value, axis, by):
    size = lax.axis_size(axis)
    pairs = [(i, i + by) for i in range(size) if 0 <= i + by < size]
    return lax.ppermute(value, axis, pairs)


def rotary_tables(seq_len):
    positions = jnp.arange(seq_len, dtype=F32)
    inverse = 1.0 / ROTARY_BASE ** (jnp.arange(0, ROTARY, 2, dtype=F32) / ROTARY)
    angles = inverse[:, None] * positions[None, :]
    return jnp.cos(angles), jnp.sin(angles)


def summed(share):
    part = lax.psum_scatter(share.astype(BF16), "dp", scatter_dimension=0, tiled=True)
    return lax.psum(part, "replica").astype(F32)


def body(tokens, cotangent, lengths, *weights):
    weights = tuple(array if array.ndim == 2 else array[0] for array in weights)
    micros = lengths.shape[0]
    width = tokens.shape[1]
    rows = tokens.shape[0] // micros
    sections = lax.axis_size("section")
    inputs = tokens.reshape(micros, rows, width)
    cotans = cotangent.reshape(micros, rows, width)
    tables = rotary_tables(rows)

    stash, received, passed = None, inputs[0], []
    for moment in range(micros + sections - 1):
        sent, stash = forward_call(moment, lengths, inputs, received, weights, tables, stash)
        if moment < micros:
            received = shifted(sent, "section", 1)
            passed.append(received)

    kept, received = None, cotans[0]
    for moment in range(micros + sections - 1):
        sent, kept = backward_call(
            moment, lengths, cotans, received, inputs, passed, weights, tables, stash, kept
        )
        if moment < micros:
            received = shifted(sent, "section", -1)

    outputs, attn_in, mlp_in, _, _, _, _, context, hidden, _ = stash
    grad_in, grad_heads, grad_up, grad_out, vectors = kept
    vector_sums = jnp.sum(vectors, axis=0)
    totals = (
        vector_sums[0],
        vector_sums[1],
        jnp.einsum("mdr,mer->de", attn_in, grad_heads, preferred_element_type=F32),
        vector_sums[4:7].reshape(-1),
        jnp.einsum("mer,mrd->ed", context, grad_out, preferred_element_type=F32),
        vector_sums[7],
        vector_sums[2],
        vector_sums[3],
        jnp.einsum("mdr,mrf->df", mlp_in, grad_up, preferred_element_type=F32),
        vector_sums[8:12].reshape(-1),
        jnp.einsum("mfr,mrd->fd", hidden, grad_out, preferred_element_type=F32),
        vector_sums[7],
    )
    grad_scale = float(tokens.shape[0] * lax.axis_size("dp") * lax.axis_size("replica")) ** (-0.5)
    scaled = tuple(summed(total)[None] * grad_scale for total in totals)
    return (outputs.reshape(1, micros * rows, width), grad_in.reshape(1, micros * rows, width), *scaled)


def solution(mesh):
    rows = P(("dp", "replica"), None)
    vector, matrix = P("section", None), P("section", None, None)
    out_rows = P("section", ("dp", "replica"), None)
    vector_out, matrix_out = P("section", "dp"), P("section", "dp", None)
    return jax.shard_map(
        body,
        mesh=mesh,
        in_specs=(
            rows, rows, P(("dp", "replica")), vector, vector, matrix, vector, matrix, vector, vector, vector, matrix,
            vector, matrix, vector,
        ),
        out_specs=(
            out_rows, out_rows, vector_out, vector_out, matrix_out, vector_out, matrix_out, vector_out, vector_out,
            vector_out, matrix_out, vector_out, matrix_out, vector_out,
        ),
        check_vma=False,
    )
```

time: 991 us -> 582 us (0.59)
  matrix products: 237 us -> 32.2 us
  waiting for transfers between devices: 476 us -> 359 us
  Pallas kernels: 0 us -> 113 us
  other arithmetic: 110 us -> 9.26 us
  local copies, waits for them, and re-layouts: 98.2 us -> 12.7 us
    dot_general x38 -> x4, matrix products: 237 us -> 32.2 us  [the longest x1 11.2 us: body(): jnp.einsum('mfr,mrd->fd', hidden, grad_out, preferred_element_type=F32)]
    pallas_call x0 -> x6, Pallas kernels: none -> 113 us  [the longest x3 58.5 us: forward_call(): pl.pallas_call(functools.partial(forward_kernel, moment, micros, len(kept...]
    ppermute x4, waiting for transfers between devices: 157 us -> 51.4 us  [shifted(): return lax.ppermute(value, axis, pairs)]
    convert_element_type x34 -> x0, other arithmetic: 40.6 us -> none  [the longest x2 14 us: layer_backward(): grad_scores = (probs_blk * (grad_probs - inner_sum)).astype(jnp.bfloat16)]
    dynamic_update_slice x14 -> x0, other arithmetic: 23.3 us -> none  [the longest x12 17.1 us: forward_step(): lax.dynamic_update_index_in_dim(buffer, newest, slot_index, 0)]
    broadcast_in_dim x10 -> x0, local copies, waits for them, and re-layouts: 23.2 us -> none  [the longest x6 12.5 us: body(): jnp.zeros(weight_arr.shape, jnp.float32)]
    another operation x19 -> x0, local copies, waits for them, and re-layouts: 20.7 us -> none
    reduce_sum x10 -> x1, other arithmetic: 17.4 us -> 0.01 us  [body(): vector_sums = jnp.sum(vectors, axis=0)]
  transfers between devices with their start and end apart: 9 -> 9, of which waited for: 9 -> 9; matrix products, arithmetic and copies ran while one was open for 2% -> 6% of each run, Pallas kernels for 0% -> 0%
where the time goes in v1:
time: 582 us; the launch traced here: 578 us
  waiting for transfers between devices  359 us (62%)
  Pallas kernels  113 us (19%)
  matrix products  32.2 us (6%)
  blocking collectives  28.7 us (5%)
  between operations  16.2 us (3%)
  local copies, waits for them, and re-layouts  12.7 us (2%)
  other arithmetic  9.26 us (2%)
  starting transfers between devices  6.7 us (1%)
    reduce_scatter x4, waiting for transfers between devices, summed(): lax.psum_scatter(share.astype(BF16), 'dp', scatter_dimension=0, tiled=True)  244 us
    psum x1, waiting for transfers between devices, summed(): return lax.psum(part, 'replica').astype(F32)  63.1 us
    pallas_call x3, Pallas kernels, forward_call(): pl.pallas_call(functools.partial(forward_kernel, moment, micros, len(kept...  58.5 us
    pallas_call x3, Pallas kernels, backward_call(): pl.pallas_call(functools.partial(backward_kernel, moment, micros, len(kep...  54.9 us
    ppermute x4, waiting for transfers between devices, shifted(): return lax.ppermute(value, axis, pairs)  51.4 us
    unnamed x1, blocking collectives  18.2 us
  transfers between devices with their start and end apart: 9, of which 9 were waited for; matrix products, arithmetic and copies ran while one was open for 6% of the time, Pallas kernels for 0%

profile of v1, /device:TPU:0, one launch (start us, length us, event | category | flops | bytes accessed | tf_op | source)
XLA Modules:
  0.0 577.7 jit_solution(18305566595791446929)
XLA Ops:
  7.2 0.8 fusion
  8.0 2.1 slice.37.refs_2_
  10.1 25.4 %layer_forward.3 = (bf16[512,768]{1,0:T(8,128)(2,1)}, bf16[2,512,768]{2,1,0:T(8,128)(2,1)}, bf16[2,768,512]{2,1,0:T(8,128)(2,1)}, bf16[2,768,512]{2,1,0:T(8,128)...) custom-call(s32[2]{0:T(128)} %refs_0_.11, ...), custom_call_target="tpu_custom_call" | custom-call | flops 8053063680 | bytes 41943040 | tf_op jit(solution)/shard_map/layer_forward/pallas_call | solution.py:219
  35.5 1.3 collective-permute-start
  36.9 2.1 collective-permute-done.refs_2_.refs_4_
  38.9 0.9 copy-done.2
  39.8 25.0 %layer_forward.4 = (bf16[512,768]{1,0:T(8,128)(2,1)}, bf16[2,512,768]{2,1,0:T(8,128)(2,1)}, bf16[2,768,512]{2,1,0:T(8,128)(2,1)}, bf16[2,768,512]{2,1,0:T(8,128)...) custom-call(s32[2]{0:T(128)} %refs_0_.11, ...), custom_call_target="tpu_custom_call", output_to_operand_aliasing={{1}: (17, {}), {2}: (18, {}), {3}: (19, {}), {4}: (20, {}),... | custom-call | flops 8053063680 | bytes 41943040 | tf_op jit(solution)/shard_map/layer_forward/pallas_call | solution.py:219
  64.8 2.3 collective-permute-start.1
  67.2 0.9 slice.38.refs_2_
  68.1 1.1 collective-permute-done.1.refs_2_.refs_5_
  69.2 0.9 copy-done.3
  70.1 8.0 %layer_forward.5 = (bf16[512,768]{1,0:T(8,128)(2,1)}, bf16[2,512,768]{2,1,0:T(8,128)(2,1)}, bf16[2,768,512]{2,1,0:T(8,128)(2,1)}, bf16[2,768,512]{2,1,0:T(8,128)...) custom-call(s32[2]{0:T(128)} %refs_0_.11, ...), custom_call_target="tpu_custom_call", output_to_operand_aliasing={{1}: (17, {}), {2}: (18, {}), {3}: (19, {}), {4}: (20, {}),... | custom-call | flops 8053063680 | bytes 41943040 | tf_op jit(solution)/shard_map/layer_forward/pallas_call | solution.py:219
  78.2 1.1 layer_backward.3
  79.2 1.3 collective-permute-start.2
  80.5 45.2 %collective-permute-done.2.refs_2_ = bf16[512,768]{1,0:T(8,128)(2,1)S(1)} collective-permute-done((bf16[512,768]{1,0:T(8,128)(2,1)}, bf16[512,768]{1,0:T(8,128)(2,1)S(1)}, u32[]{:S(2)}, u32[]{:S(2)}) %collective-permute-start.2) | collective-permute-done | bytes 786464 | tf_op jit(solution)/shard_map/ppermute | solution.py:508
  125.7 0.9 copy-done.11
  126.6 26.8 %layer_backward.4 = (bf16[512,768]{1,0:T(8,128)(2,1)}, f32[2,512,768]{2,1,0:T(8,128)}, bf16[2,2304,512]{2,1,0:T(8,128)(2,1)}, bf16[2,512,3072]{2,1,0:T(8,128)(2,...) custom-call(s32[2]{0:T(128)} %refs_0_.11, ...), custom_call_target="tpu_custom_call", output_to_operand_aliasing={{1}: (20, {}), {2}: (21, {}), {3}: (22, {}), {4}: (23, {}),... | custom-call | flops 8858370048 | bytes 41943040 | tf_op jit(solution)/shard_map/layer_backward/pallas_call | solution.py:460
  153.4 1.3 collective-permute-start.3
  154.7 3.1 collective-permute-done.3.refs_2_
  157.8 0.9 copy-done.10
  158.7 27.0 %layer_backward.5 = (bf16[512,768]{1,0:T(8,128)(2,1)}, f32[2,512,768]{2,1,0:T(8,128)}, bf16[2,2304,512]{2,1,0:T(8,128)(2,1)}, bf16[2,512,3072]{2,1,0:T(8,128)(2,...) custom-call(s32[2]{0:T(128)} %refs_0_.11, ...), custom_call_target="tpu_custom_call", output_to_operand_aliasing={{1}: (20, {}), {2}: (21, {}), {3}: (22, {}), {4}: (23, {}),... | custom-call | flops 8858370048 | bytes 41943040 | tf_op jit(solution)/shard_map/layer_backward/pallas_call | solution.py:460
  185.7 3.9 bitcast_convert_fusion.3
  189.7 7.6 %bitcast_convert_fusion.2 = bf16[768,2304]{1,0:T(8,128)(2,1)} fusion(bf16[2,768,512]{2,1,0:T(8,128)(2,1)S(1)} %copy-done.4, bf16[2,2304,512]{2,1,0:T(8,128)(2,1)} %get-tuple-element.107), kind=kOutput, calls=%fused_computation.2 | convolution fusion | flops 3625648128 | bytes 9830400 | tf_op jit(solution)/shard_map/mdr,mer->de/dot_general | solution.py:554
  197.4 0.3 reduce-scatter.11.cloned.1.call-start
  197.7 1.2 copy-done.6
  198.9 11.2 %bitcast_convert_fusion = bf16[3072,768]{1,0:T(8,128)(2,1)} fusion(bf16[2,3072,512]{2,1,0:T(8,128)(2,1)} %get-tuple-element.111, bf16[2,512,768]{2,1,0:T(8,128)(2,1)S(1)} %copy-done.6), kind=kOutput, calls=%fused_computation | convolution fusion | flops 4834197504 | bytes 12582912 | tf_op jit(solution)/shard_map/mfr,mrd->fd/dot_general | solution.py:562
  210.1 1.3 copy-done.5
  211.5 9.5 %bitcast_convert_fusion.1 = bf16[768,3072]{1,0:T(8,128)(2,1)} fusion(bf16[2,768,512]{2,1,0:T(8,128)(2,1)S(1)} %copy-done.5, bf16[2,512,3072]{2,1,0:T(8,128)(2,1)} %get-tuple-element.110), kind=kOutput, calls=%fused_computation.1 | convolution fusion | flops 4834197504 | bytes 12582912 | tf_op jit(solution)/shard_map/mdr,mrf->df/dot_general | solution.py:560
  221.0 0.7 reduce-scatter.7.cloned.1.call-done
  221.7 67.4 %reduce-scatter.5.cloned.1.call-done = bf16[192,2304]{1,0:T(8,128)(2,1)} async-done(((bf16[768,2304]{1,0:T(8,128)(2,1)}), bf16[192,2304]{1,0:T(8,128)(2,1)}) %reduce-scatter.5.cloned.1.call-update) | async-done | bytes 884752 | tf_op jit(solution)/shard_map/reduce_scatter | solution.py:519
  289.1 87.9 %reduce-scatter.11.cloned.1.call-done = bf16[768,768]{1,0:T(8,128)(2,1)} async-done(((bf16[3072,768]{1,0:T(8,128)(2,1)}), bf16[768,768]{1,0:T(8,128)(2,1)}) %reduce-scatter.11.cloned.1.call-update) | async-done | bytes 1179664 | tf_op jit(solution)/shard_map/reduce_scatter | solution.py:519
  377.0 88.0 %reduce-scatter.9.cloned.1.call-done = bf16[192,3072]{1,0:T(8,128)(2,1)} async-done(((bf16[768,3072]{1,0:T(8,128)(2,1)}), bf16[192,3072]{1,0:T(8,128)(2,1)}) %reduce-scatter.9.cloned.1.call-update) | async-done | bytes 1179664 | tf_op jit(solution)/shard_map/reduce_scatter | solution.py:519
  465.0 0.6 copy-done.14
  465.6 0.6 dynamic-slice
  468.3 18.2 %all-reduce.9 = (bf16[768]{0:T(1024)(128)(2,1)S(1)}, bf16[768]{0:T(1024)(128)(2,1)S(1)}, bf16[2304]{0:T(1024)(128)(2,1)S(1)}, bf16[768]{0:T(1024)(128)(2,1)S(1)}...) all-reduce(bf16[768]{0:T(1024)(128)(2,1)S(1)} %get-tuple-element.11, ...), channel_id=2, replica_groups=mesh['section'=2,'dp'=4,'replica'=4] {'dp'}, use_global_device_ids=true, to_apply=%region_1.0.clone | all-reduce | flops 9216 | bytes 36864
  486.9 0.1 dynamic-slice.13
  487.0 10.5 %all-reduce.7 = (bf16[192]{0:T(256)(128)(2,1)S(1)}, bf16[192]{0:T(256)(128)(2,1)S(1)}, bf16[576]{0:T(1024)(128)(2,1)S(1)}, bf16[192]{0:T(256)(128)(2,1)S(1)}, bf...) all-reduce(bf16[192]{0:T(256)(128)(2,1)S(1)} %dynamic-slice.1, ...), channel_id=1, replica_groups=mesh['section'=2,'dp'=4,'replica'=4] {'replica'}, use_global_device_ids=true, to_apply=%region_2.0 | all-reduce | flops 2304 | bytes 9216 | tf_op jit(solution)/shard_map/psum | solution.py:520
  497.5 0.6 mul.193
  498.1 0.6 mul.178
  498.7 0.6 convert_multiply_fusion.4
  499.3 0.6 convert_multiply_fusion.6
  499.8 0.6 convert_multiply_fusion.2
  500.4 63.1 %all-reduce.12.cloned.1.call-done = (bf16[192,2304]{1,0:T(8,128)(2,1)}, bf16[192,768]{1,0:T(8,128)(2,1)}, bf16[192,3072]{1,0:T(8,128)(2,1)}, bf16[768,768]{1,0:T(8,128)(2,1)}) async-done(((bf16[192,2304]{1,0:T(8,128)(2,1)}, bf16[192,768]{1,0:T(8,128)(2,1)}, bf16[192,3072]{1,0:T(8,128)(2,1)}, bf16[768,768]{1,0:T(8,128)(2,1)}), (bf16[192,2304]{1,0:T(8,128)(2,1)}, bf16[192,768]{1,0:T(8,128)(2,1)}, ...) | async-done | bytes 3538960 | tf_op jit(solution)/shard_map/psum | solution.py:520
  563.5 2.9 multiply_bitcast_fusion
  566.5 1.7 multiply_bitcast_fusion.1
  568.1 1.3 multiply_bitcast_fusion.2
  569.5 0.9 multiply_bitcast_fusion.3
  570.3 0.6 copy.94
  (47 shorter events, 0.9 us)
Async XLA Ops:
  7.2 214.5 %reduce-scatter.7.cloned.1.call-start = ((), (), s32[]{:S(2)}) async-start(), calls=%async_computation.5 | async-start | bytes 1474560 | tf_op jit(solution)/shard_map/reduce_scatter | solution.py:519
  35.5 3.4 collective-permute-start
  38.9 0.9 copy-start.2
  39.8 27.4 %copy-start.1 = (bf16[1024,768]{1,0:T(8,128)(2,1)S(1)}, bf16[1024,768]{1,0:T(8,128)(2,1)}, u32[]{:S(2)}) copy-start(bf16[1024,768]{1,0:T(8,128)(2,1)} %param.16) | copy-start | bytes 4718596
  64.8 4.4 collective-permute-start.1
  69.2 0.9 copy-start.3
  79.2 46.5 %collective-permute-start.2 = (bf16[512,768]{1,0:T(8,128)(2,1)}, bf16[512,768]{1,0:T(8,128)(2,1)S(1)}, u32[]{:S(2)}, u32[]{:S(2)}) collective-permute-start(bf16[512,768]{1,0:T(8,128)(2,1)} %get-tuple-element.92), channel_id=1, source_target_pairs={{16,0},{17,1},{18,2},{19,3},{20,4},{21,5},{22,6},{23,7},{24,8},{25... | collective-permute-start | bytes 2359304 | tf_op jit(solution)/shard_map/ppermute | solution.py:508
  125.7 0.9 copy-start.11
  153.4 4.4 collective-permute-start.3
  157.8 0.9 copy-start.10
  158.7 27.0 %copy-start = (bf16[2,768,512]{2,1,0:T(8,128)(2,1)S(1)}, bf16[2,768,512]{2,1,0:T(8,128)(2,1)}, u32[]{:S(2)}) copy-start(bf16[2,768,512]{2,1,0:T(8,128)(2,1)} %get-tuple-element.90.refs_18_) | copy-start | bytes 4718596
  185.7 4.0 copy-start.4
  189.6 99.4 %reduce-scatter.5.cloned.1.call-start = ((), (), s32[]{:S(2)}) async-start(), calls=%async_computation.4 | async-start | bytes 4423680 | tf_op jit(solution)/shard_map/reduce_scatter | solution.py:519
  197.3 1.6 copy-start.6
  197.4 179.6 %reduce-scatter.11.cloned.1.call-start = ((), (), s32[]{:S(2)}) async-start(), calls=%async_computation.7 | async-start | bytes 5898240 | tf_op jit(solution)/shard_map/reduce_scatter | solution.py:519
  210.1 1.4 copy-start.5
  210.1 254.9 %reduce-scatter.9.cloned.1.call-start = ((), (), s32[]{:S(2)}) async-start(), calls=%async_computation.6 | async-start | bytes 5898240 | tf_op jit(solution)/shard_map/reduce_scatter | solution.py:519
  221.0 342.6 %all-reduce.12.cloned.1.call-start = ((), (), s32[]{:S(2)}) async-start(), calls=%async_computation.8 | async-start | bytes 7077888 | tf_op jit(solution)/shard_map/psum | solution.py:520
  465.0 0.7 copy-start.14
  465.0 3.2 copy-start.8
  499.3 71.0 %copy-start.13 = (f32[192]{0:T(256)}, f32[192]{0:T(256)S(1)}, u32[]{:S(2)}) copy-start(f32[192]{0:T(256)S(1)} %get-tuple-element.139) | copy-start | bytes 2308
  563.5 2.9 copy-start.7
  566.5 1.7 copy-start.9
  568.1 1.3 copy-start.12
Sparse Core Ops, SparseCore 0:
  189.8 31.8 reduce-scatter.6
  224.0 65.0 reduce-scatter.4
  291.4 85.5 reduce-scatter.10
  379.1 85.7 reduce-scatter.8
  468.3 95.2 all-reduce.11

commit v2 on v1

--- a/solution.py
+++ b/solution.py
@@ -23,6 +23,7 @@
 ROW_CHUNK = 128
 QKV_TILE = 256
 FF_TILE = 512
+PIECE = 384
 
 
 def dims_dot(left, right, left_dim, right_dim):
@@ -502,6 +503,326 @@
     return results[0], results[1:]
 
 
+def partner(axis, bit):
+    index = lax.axis_index(axis)
+    own_bit = (index // bit) % 2
+    return {axis: index + bit - 2 * bit * own_bit}, own_bit
+
+
+def piece_plan(width, hidden_width, piece):
+    counts = [width // piece, hidden_width // piece, hidden_width // piece, 3 * width // piece]
+    starts = [0]
+    for count in counts:
+        starts.append(starts[-1] + count)
+    return starts
+
+
+def reduce_kernel(bits, piece, *refs):
+    (
+        context_h, hidden_h, mlp_in_h, attn_in_h, grad_out_h, grad_up_h, grad_heads_h, vectors_h,
+        qkv_o, out_o, up_o, down_o, vectors_o,
+        left, right, heads, vectors, own, final, from_first, *rest,
+    ) = refs
+    from_dp, rest = rest[:bits], rest[bits:]
+    (
+        from_second, vector_sum, from_vector,
+        in_sems, send_sems, recv_sems, vector_send, vector_recv, out_sems,
+    ) = rest
+    micros, devices, share, rows = attn_in_h.shape
+    width = devices * share
+    hidden_width = grad_up_h.shape[2]
+    groups = hidden_width // width
+    out_at, down_at, up_at, qkv_at, pieces = piece_plan(width, hidden_width, piece)
+    across = width // piece
+
+    barrier = pltpu.get_barrier_semaphore()
+    dp_peers = [partner("dp", 1 << bit) for bit in range(bits)]
+    replica_peers = [partner("replica", 1), partner("replica", 2)]
+    for device, _ in dp_peers + replica_peers:
+        pl.semaphore_signal(barrier, inc=1, device_id=device, device_id_type=pl.DeviceIdType.MESH)
+
+    wide = hidden_width + width
+    loads = [
+        [(context_h, left.at[0]), (grad_out_h, right.at[:, :, 0:width]), (vectors_h, vectors)],
+        [(hidden_h.at[:, :, group], left.at[3 + group]) for group in range(groups)],
+        [(mlp_in_h, left.at[1]), (grad_up_h, right.at[:, :, width:wide])],
+        [(attn_in_h, left.at[2]), (grad_heads_h, heads)],
+    ]
+    copies, count = [], 0
+    for group in loads:
+        copies.append([])
+        for src, dst in group:
+            copies[-1].append(pltpu.make_async_copy(src, dst, in_sems.at[count]))
+            count += 1
+    for copy in copies[0]:
+        copy.start()
+    for copy in copies[0]:
+        copy.wait()
+    for group in copies[1:]:
+        for copy in group:
+            copy.start()
+    vector_sum[0] = jnp.sum(vectors[...], axis=0)
+    pl.semaphore_wait(barrier, len(dp_peers) + len(replica_peers))
+
+    dp_bits = [own_bit for _, own_bit in dp_peers]
+
+    def keep(k, depth, first_bit=None, second_bit=None, flip=None):
+        index = [k] + [slice(None)] * (bits - depth)
+        for bit in reversed(range(depth)):
+            index.append(1 - dp_bits[bit] if flip == bit else dp_bits[bit])
+        if first_bit is not None:
+            index.append(first_bit)
+        if second_bit is not None:
+            index.append(second_bit)
+        return tuple(index)
+
+    def transfers(k, turned):
+        (first, first_bit), (second, second_bit) = replica_peers[::-1] if turned else replica_peers
+        steps = [
+            (own.at[keep(k, 0, 1 - first_bit)], from_first.at[k], first, own.at[keep(k, 0, first_bit)]),
+        ]
+        for bit in range(bits):
+            steps.append(
+                (
+                    own.at[keep(k, bit + 1, first_bit, flip=bit)],
+                    from_dp[bit].at[k],
+                    dp_peers[bit][0],
+                    own.at[keep(k, bit + 1, first_bit)],
+                )
+            )
+        mine = final.at[k, first_bit, second_bit]
+        steps.append(
+            (
+                own.at[keep(k, bits, first_bit, 1 - second_bit)],
+                from_second.at[k],
+                second,
+                own.at[keep(k, bits, first_bit, second_bit)],
+            )
+        )
+        steps.append((mine, mine, second, None))
+        steps.append((final.at[k, first_bit], final.at[k, first_bit], first, None))
+        return steps, mine
+
+    def copy_of(k, stage, step):
+        src, dst, device, _ = step
+        return pltpu.make_async_remote_copy(
+            src_ref=src,
+            dst_ref=dst,
+            send_sem=send_sems.at[k, stage],
+            recv_sem=recv_sems.at[k, stage],
+            device_id=device,
+            device_id_type=pl.DeviceIdType.MESH,
+        )
+
+    n_steps = bits + 4
+
+    def advance(k, stage, turned):
+        steps, mine = transfers(k, turned)
+        if stage > 0:
+            step = steps[stage - 1]
+            copy_of(k, stage - 1, step).wait()
+            if step[3] is not None:
+                total = step[3][...].astype(F32) + step[1][...].astype(F32)
+                if stage == bits + 2:
+                    mine[...] = total.astype(BF16)
+                else:
+                    step[3][...] = total.astype(BF16)
+        if stage < n_steps:
+            copy_of(k, stage, steps[stage]).start()
+
+    def advance_either(k, stage):
+        for turned in (False, True):
+
+            @pl.when(k % 2 == int(turned))
+            def _():
+                advance(k, stage, turned)
+
+    shape = own.shape[1:]
+
+    def panel(index, micro):
+        return left[index, micro].reshape(width, rows)
+
+    def set_own(k, index, columns):
+        value = columns(0, panel(index, 0))
+        for micro in range(1, micros):
+            value = value + columns(micro, panel(index, micro))
+        own[k] = value.astype(BF16).reshape(shape)
+
+    def lanes(index):
+        return pl.ds(pl.multiple_of(index * piece, 128), piece)
+
+    def compute(k):
+        @pl.when(k < down_at)
+        def _():
+            part = lanes(k)
+            set_own(k, 0, lambda micro, block: dims_dot(block, right[micro, :, part], 1, 0))
+
+        @pl.when((k >= down_at) & (k < up_at))
+        def _():
+            part = lanes((k - down_at) % across)
+            set_own(
+                k, 3 + (k - down_at) // across, lambda micro, block: dims_dot(block, right[micro, :, part], 1, 0)
+            )
+
+        @pl.when((k >= up_at) & (k < qkv_at))
+        def _():
+            part = lanes(across + k - up_at)
+            set_own(k, 1, lambda micro, block: dims_dot(block, right[micro, :, part], 1, 0))
+
+        @pl.when(k >= qkv_at)
+        def _():
+            part = lanes(k - qkv_at)
+            set_own(k, 2, lambda micro, block: dims_dot(block, heads[micro, part, :], 1, 1))
+
+    def out_copy(k, kind):
+        if kind == "down":
+            target = down_o.at[(k - down_at) // across, :, :, :, lanes((k - down_at) % across)]
+        else:
+            ref, start = {"out": (out_o, out_at), "up": (up_o, up_at), "qkv": (qkv_o, qkv_at)}[kind]
+            target = ref.at[:, :, :, lanes(k - start)]
+        return pltpu.make_async_copy(final.at[k], target, out_sems.at[k])
+
+    ranges = {"out": (out_at, down_at), "down": (down_at, up_at), "up": (up_at, qkv_at), "qkv": (qkv_at, pieces)}
+
+    def stored(k, do):
+        for kind, (first, end) in ranges.items():
+
+            @pl.when((k >= first) & (k < end))
+            def _():
+                do(out_copy(k, kind))
+
+    vector_peers = dp_peers + replica_peers
+
+    def vector_copy(i):
+        return pltpu.make_async_remote_copy(
+            src_ref=vector_sum.at[i],
+            dst_ref=from_vector.at[i],
+            send_sem=vector_send.at[i],
+            recv_sem=vector_recv.at[i],
+            device_id=vector_peers[i][0],
+            device_id_type=pl.DeviceIdType.MESH,
+        )
+
+    lags = [0]
+    for stage in range(n_steps):
+        lags.append(lags[-1] + (4 if stage == 0 else 2))
+
+    def turn(t, carry):
+        for at, group in zip((down_at, up_at, qkv_at), copies[1:]):
+
+            @pl.when(t == at)
+            def _():
+                for copy in group:
+                    copy.wait()
+
+        @pl.when(t < pieces)
+        def _():
+            compute(t)
+
+        for stage in range(n_steps + 1):
+            k = t - lags[stage]
+
+            @pl.when((k >= 0) & (k < pieces))
+            def _():
+                advance_either(k, stage)
+                if stage == n_steps:
+                    stored(k, lambda copy: copy.start())
+
+        for i in range(len(vector_peers) + 1):
+
+            @pl.when(t == 4 * i)
+            def _():
+                if i > 0:
+                    vector_copy(i - 1).wait()
+                    vector_sum[i] = vector_sum[i - 1] + from_vector[i - 1]
+                if i < len(vector_peers):
+                    vector_copy(i).start()
+                else:
+                    pltpu.make_async_copy(vector_sum.at[i], vectors_o, out_sems.at[pieces]).start()
+
+        return carry
+
+    lax.fori_loop(0, pieces + lags[-1], turn, 0)
+
+    def finish(k, carry):
+        stored(k, lambda copy: copy.wait())
+        return carry
+
+    lax.fori_loop(0, pieces, finish, 0)
+    pltpu.make_async_copy(vector_sum.at[len(vector_peers)], vectors_o, out_sems.at[pieces]).wait()
+
+
+def reduce_call(stash, kept):
+    _, attn_in, mlp_in, _, _, _, _, context, hidden, _ = stash
+    _, grad_heads, grad_up, grad_out, vectors = kept
+    micros, width, rows = attn_in.shape
+    hidden_width = hidden.shape[1]
+    groups = hidden_width // width
+    devices = lax.axis_size("dp")
+    bits = devices.bit_length() - 1
+    share, quarter = width // devices, width // devices // 4
+    piece = PIECE
+    pieces = piece_plan(width, hidden_width, piece)[-1]
+    loads = 6 + groups + 1
+    tall = (micros, devices, share, rows)
+    halves = [2] * bits
+    steps = bits + 4
+    peers = bits + 2
+    shape = lambda columns: jax.ShapeDtypeStruct((2, 2, quarter, columns), BF16)
+    outs = pl.pallas_call(
+        functools.partial(reduce_kernel, bits, piece),
+        out_shape=[
+            shape(3 * width),
+            shape(width),
+            shape(hidden_width),
+            jax.ShapeDtypeStruct((groups, 2, 2, quarter, width), BF16),
+            jax.ShapeDtypeStruct(vectors.shape[1:], F32),
+        ],
+        in_specs=[ANY] * 8,
+        out_specs=[ANY] * 5,
+        scratch_shapes=[
+            pltpu.VMEM((3 + groups, *tall), BF16),
+            pltpu.VMEM((micros, rows, width + hidden_width), BF16),
+            pltpu.VMEM(grad_heads.shape, BF16),
+            pltpu.VMEM(vectors.shape, F32),
+            pltpu.VMEM((pieces, *halves, 2, 2, quarter, piece), BF16),
+            pltpu.VMEM((pieces, 2, 2, quarter, piece), BF16),
+            pltpu.VMEM((pieces, *halves, 2, quarter, piece), BF16),
+            *[pltpu.VMEM((pieces, *halves[bit + 1 :], 2, quarter, piece), BF16) for bit in range(bits)],
+            pltpu.VMEM((pieces, quarter, piece), BF16),
+            pltpu.VMEM((peers + 1, *vectors.shape[1:]), F32),
+            pltpu.VMEM((peers, *vectors.shape[1:]), F32),
+            pltpu.SemaphoreType.DMA((loads,)),
+            pltpu.SemaphoreType.DMA((pieces, steps)),
+            pltpu.SemaphoreType.DMA((pieces, steps)),
+            pltpu.SemaphoreType.DMA((peers,)),
+            pltpu.SemaphoreType.DMA((peers,)),
+            pltpu.SemaphoreType.DMA((pieces + 1,)),
+        ],
+        compiler_params=pltpu.CompilerParams(
+            collective_id=0, has_side_effects=True, vmem_limit_bytes=60 << 20
+        ),
+        cost_estimate=pl.CostEstimate(
+            flops=2 * micros * rows * width * (4 * width + 2 * hidden_width),
+            bytes_accessed=30 << 20,
+            transcendentals=0,
+        ),
+        name="weight_gradients",
+    )(
+        context.reshape(tall),
+        hidden.reshape(micros, devices, groups, share, rows),
+        mlp_in.reshape(tall),
+        attn_in.reshape(tall),
+        grad_out,
+        grad_up,
+        grad_heads,
+        vectors,
+    )
+    qkv, out, up, down, sums = outs
+    scattered = [array.reshape(-1, array.shape[-1]) for array in (qkv, out, up, down)]
+    return scattered, sums
+
+
 def shifted(value, axis, by):
     size = lax.axis_size(axis)
     pairs = [(i, i + by) for i in range(size) if 0 <= i + by < size]
@@ -518,6 +839,32 @@
 def summed(share):
     part = lax.psum_scatter(share.astype(BF16), "dp", scatter_dimension=0, tiled=True)
     return lax.psum(part, "replica").astype(F32)
+
+
+def in_pieces(width):
+    devices = lax.axis_size("dp")
+    return devices & (devices - 1) == 0 and lax.axis_size("replica") == 4 and width % (64 * devices) == 0
+
+
+def local_totals(stash, kept):
+    _, attn_in, mlp_in, _, _, _, _, context, hidden, _ = stash
+    _, grad_heads, grad_up, grad_out, vectors = kept
+    vector_sums = jnp.sum(vectors, axis=0)
+    groups = hidden.shape[1] // attn_in.shape[1]
+    return (
+        vector_sums[0],
+        vector_sums[1],
+        jnp.einsum("mdr,mer->de", attn_in, grad_heads, preferred_element_type=F32),
+        vector_sums[4:7].reshape(-1),
+        jnp.einsum("mer,mrd->ed", context, grad_out, preferred_element_type=F32),
+        vector_sums[7],
+        vector_sums[2],
+        vector_sums[3],
+        jnp.einsum("mdr,mrf->df", mlp_in, grad_up, preferred_element_type=F32),
+        vector_sums[8 : 8 + groups].reshape(-1),
+        jnp.einsum("mfr,mrd->fd", hidden, grad_out, preferred_element_type=F32),
+        vector_sums[7],
+    )
 
 
 def body(tokens, cotangent, lengths, *weights):
@@ -545,26 +892,25 @@
         if moment < micros:
             received = shifted(sent, "section", -1)
 
-    outputs, attn_in, mlp_in, _, _, _, _, context, hidden, _ = stash
-    grad_in, grad_heads, grad_up, grad_out, vectors = kept
-    vector_sums = jnp.sum(vectors, axis=0)
-    totals = (
-        vector_sums[0],
-        vector_sums[1],
-        jnp.einsum("mdr,mer->de", attn_in, grad_heads, preferred_element_type=F32),
-        vector_sums[4:7].reshape(-1),
-        jnp.einsum("mer,mrd->ed", context, grad_out, preferred_element_type=F32),
-        vector_sums[7],
-        vector_sums[2],
-        vector_sums[3],
-        jnp.einsum("mdr,mrf->df", mlp_in, grad_up, preferred_element_type=F32),
-        vector_sums[8:12].reshape(-1),
-        jnp.einsum("mfr,mrd->fd", hidden, grad_out, preferred_element_type=F32),
-        vector_sums[7],
-    )
     grad_scale = float(tokens.shape[0] * lax.axis_size("dp") * lax.axis_size("replica")) ** (-0.5)
-    scaled = tuple(summed(total)[None] * grad_scale for total in totals)
-    return (outputs.reshape(1, micros * rows, width), grad_in.reshape(1, micros * rows, width), *scaled)
+    if in_pieces(width):
+        matrices, vectors = reduce_call(stash, kept)
+        mine = lax.axis_index("dp")
+        devices = lax.axis_size("dp")
+
+        def slice_of(first, count):
+            size = count * width // devices
+            return lax.dynamic_slice_in_dim(vectors[first : first + count].reshape(-1), mine * size, size)
+
+        down_bias = slice_of(7, 1)
+        shares = (
+            slice_of(0, 1), slice_of(1, 1), matrices[0], slice_of(4, 3), matrices[1], down_bias, slice_of(2, 1),
+            slice_of(3, 1), matrices[2], slice_of(8, weights[8].shape[1] // width), matrices[3], down_bias,
+        )
+    else:
+        shares = tuple(summed(total) for total in local_totals(stash, kept))
+    scaled = tuple(share.astype(F32)[None] * grad_scale for share in shares)
+    return (stash[0].reshape(1, micros * rows, width), kept[0].reshape(1, micros * rows, width), *scaled)
 
 
 def solution(mesh):

time: 582 us -> 320 us (0.55)
  waiting for transfers between devices: 359 us -> 51.3 us
  Pallas kernels: 113 us -> 237 us
  matrix products: 32.2 us -> 0 us
  blocking collectives: 28.7 us -> 0 us
  between operations: 16.2 us -> 0.96 us
    reduce_scatter x4 -> x0, waiting for transfers between devices: 244 us -> none  [summed(): lax.psum_scatter(share.astype(BF16), 'dp', scatter_dimension=0, tiled=True)]
    pallas_call x0 -> x1, Pallas kernels: none -> 124 us  [reduce_call(): pl.pallas_call(functools.partial(reduce_kernel, bits, piece), out_shape=[...]
    psum x1 -> x0, waiting for transfers between devices: 63.1 us -> none  [summed(): return lax.psum(part, 'replica').astype(F32)]
    dot_general x4 -> x0, matrix products: 32.2 us -> none  [the longest x1 11.2 us: body(): jnp.einsum('mfr,mrd->fd', hidden, grad_out, preferred_element_type=F32)]
    unnamed x1 -> x0, blocking collectives: 18.2 us -> none
    psum x1 -> x0, blocking collectives: 10.5 us -> none  [summed(): return lax.psum(part, 'replica').astype(F32)]
  transfers between devices with their start and end apart: 9 -> 4, of which waited for: 9 -> 4; matrix products, arithmetic and copies ran while one was open for 6% -> 0% of each run, Pallas kernels for 0% -> 0%
where the time goes in v2:
time: 320 us; the launch traced here: 316 us
  Pallas kernels  237 us (74%)
  waiting for transfers between devices  51.3 us (16%)
  local copies, waits for them, and re-layouts  10.7 us (3%)
  other arithmetic  9.72 us (3%)
  starting transfers between devices  6.24 us (2%)
    pallas_call x1, Pallas kernels, reduce_call(): pl.pallas_call(functools.partial(reduce_kernel, bits, piece), out_shape=[...  124 us
    pallas_call x3, Pallas kernels, forward_call(): pl.pallas_call(functools.partial(forward_kernel, moment, micros, len(kept...  58.6 us
    pallas_call x3, Pallas kernels, backward_call(): pl.pallas_call(functools.partial(backward_kernel, moment, micros, len(kep...  55.3 us
    ppermute x4, waiting for transfers between devices, shifted(): return lax.ppermute(value, axis, pairs)  51.3 us
    mul x9, other arithmetic, body(): scaled = tuple((share.astype(F32)[None] * grad_scale for share in shares))  8.96 us
  transfers between devices with their start and end apart: 4, of which 4 were waited for; matrix products, arithmetic and copies ran while one was open for 0% of the time, Pallas kernels for 0%

profile of v2, /device:TPU:0, one launch (start us, length us, event | category | flops | bytes accessed | tf_op | source)
XLA Modules:
  0.0 316.4 jit_solution(11451909649741025130)
XLA Ops:
  0.7 0.8 fusion
  1.4 2.1 slice.29.refs_2_
  3.5 25.1 %layer_forward.3 = (bf16[512,768]{1,0:T(8,128)(2,1)}, bf16[2,512,768]{2,1,0:T(8,128)(2,1)}, bf16[2,768,512]{2,1,0:T(8,128)(2,1)}, bf16[2,768,512]{2,1,0:T(8,128)...) custom-call(s32[2]{0:T(128)} %refs_0_.11, ...), custom_call_target="tpu_custom_call" | custom-call | flops 8053063680 | bytes 41943040 | tf_op jit(solution)/shard_map/layer_forward/pallas_call | solution.py:220
  28.6 1.3 collective-permute-start
  30.0 2.1 collective-permute-done.refs_2_.refs_4_
  32.0 0.0 copy-start.1
  32.0 0.9 copy-done.1
  32.9 0.0 copy-start
  32.9 25.6 %layer_forward.4 = (bf16[512,768]{1,0:T(8,128)(2,1)}, bf16[2,512,768]{2,1,0:T(8,128)(2,1)}, bf16[2,768,512]{2,1,0:T(8,128)(2,1)}, bf16[2,768,512]{2,1,0:T(8,128)...) custom-call(s32[2]{0:T(128)} %refs_0_.11, ...), custom_call_target="tpu_custom_call", output_to_operand_aliasing={{1}: (17, {}), {2}: (18, {}), {3}: (19, {}), {4}: (20, {}),... | custom-call | flops 8053063680 | bytes 41943040 | tf_op jit(solution)/shard_map/layer_forward/pallas_call | solution.py:220
  58.6 2.3 collective-permute-start.1
  60.9 0.0 copy-done
  60.9 0.9 slice.30.refs_2_
  61.8 1.1 collective-permute-done.1.refs_2_.refs_5_
  62.9 0.0 copy-start.2
  63.0 0.9 copy-done.2
  63.9 7.8 %layer_forward.5 = (bf16[512,768]{1,0:T(8,128)(2,1)}, bf16[2,512,768]{2,1,0:T(8,128)(2,1)}, bf16[2,768,512]{2,1,0:T(8,128)(2,1)}, bf16[2,768,512]{2,1,0:T(8,128)...) custom-call(s32[2]{0:T(128)} %refs_0_.11, ...), custom_call_target="tpu_custom_call", output_to_operand_aliasing={{1}: (17, {}), {2}: (18, {}), {3}: (19, {}), {4}: (20, {}),... | custom-call | flops 8053063680 | bytes 41943040 | tf_op jit(solution)/shard_map/layer_forward/pallas_call | solution.py:220
  71.6 1.1 layer_backward.3
  72.7 1.3 collective-permute-start.2
  74.0 45.1 %collective-permute-done.2.refs_2_ = bf16[512,768]{1,0:T(8,128)(2,1)S(1)} collective-permute-done((bf16[512,768]{1,0:T(8,128)(2,1)}, bf16[512,768]{1,0:T(8,128)(2,1)S(1)}, u32[]{:S(2)}, u32[]{:S(2)}) %collective-permute-start.2) | collective-permute-done | bytes 786464 | tf_op jit(solution)/shard_map/ppermute | solution.py:829
  119.1 0.0 copy-start.6
  119.1 0.9 copy-done.6
  120.0 26.9 %layer_backward.4 = (bf16[512,768]{1,0:T(8,128)(2,1)}, f32[2,512,768]{2,1,0:T(8,128)}, bf16[2,2304,512]{2,1,0:T(8,128)(2,1)}, bf16[2,512,3072]{2,1,0:T(8,128)(2,...) custom-call(s32[2]{0:T(128)} %refs_0_.11, ...), custom_call_target="tpu_custom_call", output_to_operand_aliasing={{1}: (20, {}), {2}: (21, {}), {3}: (22, {}), {4}: (23, {}),... | custom-call | flops 8858370048 | bytes 41943040 | tf_op jit(solution)/shard_map/layer_backward/pallas_call | solution.py:461
  146.9 1.3 collective-permute-start.3
  148.2 3.1 collective-permute-done.3.refs_2_
  151.3 0.0 copy-start.5
  151.3 0.9 copy-done.5
  152.2 27.3 %layer_backward.5 = (bf16[512,768]{1,0:T(8,128)(2,1)}, f32[2,512,768]{2,1,0:T(8,128)}, bf16[2,2304,512]{2,1,0:T(8,128)(2,1)}, bf16[2,512,3072]{2,1,0:T(8,128)(2,...) custom-call(s32[2]{0:T(128)} %refs_0_.11, ...), custom_call_target="tpu_custom_call", output_to_operand_aliasing={{1}: (20, {}), {2}: (21, {}), {3}: (22, {}), {4}: (23, {}),... | custom-call | flops 8858370048 | bytes 41943040 | tf_op jit(solution)/shard_map/layer_backward/pallas_call | solution.py:461
  179.5 123.6 %weight_gradients.1 = (bf16[2,2,48,2304]{3,2,1,0:T(8,128)(2,1)}, bf16[2,2,48,768]{3,2,1,0:T(8,128)(2,1)}, bf16[2,2,48,3072]{3,2,1,0:T(8,128)(2,1)}, bf16[4,2,2,48,768]{4,3,2,1,0:T(8,128)(2,1)}, f32[16,768]{1,0:T(8,128)}) custom-call(bf16[2,4,192,512]{3,2,1,0:T(8,128)(2,1)} %bitcast.40, bf16[2,4,4,192,512]{4,3,2,1,0:T(8,128)(2,1)} %bitcast.47, ...), custom_call_target="tpu_custom_call" | custom-call | flops 14495514624 | bytes 31457280 | tf_op jit(solution)/shard_map/weight_gradients/pallas_call | solution.py:772
  303.0 0.9 fusion.7
  304.0 0.7 slice.37
  304.7 0.7 slice.33
  305.5 0.6 fusion.4
  306.1 0.0 copy-start.8
  306.1 3.0 convert_multiply_fusion.1
  309.1 0.0 copy-done.3
  309.1 1.6 convert_multiply_fusion
  310.8 0.0 copy-done.4
  310.8 1.3 convert_multiply_fusion.2
  312.1 0.0 copy-done.7
  312.1 0.9 convert_multiply_fusion.3
  313.0 0.1 dynamic-slice_multiply_fusion
  313.1 0.6 mul.231
  313.7 0.1 dynamic-slice_multiply_fusion.1
  313.8 0.6 mul.218
  314.3 0.6 fusion.6
  315.0 0.6 fusion.2
  315.6 0.0 copy-done.8
  315.6 0.6 copy.90
  (6 shorter events, 0.0 us)
Async XLA Ops:
  28.6 3.4 %collective-permute-start = (bf16[512,768]{1,0:T(8,128)(2,1)}, bf16[512,768]{1,0:T(8,128)(2,1)S(1)}, u32[]{:S(2)}, u32[]{:S(2)}) collective-permute-start(bf16[512,768]{1,0:T(8,128)(2,1)} %get-tuple-element.68), channel_id=1, source_target_pairs={{0,16},{1,17},{2,18},{3,19},{4,20},{5,21},{6,22},{7,23},{8,24},{9,... | collective-permute-start | bytes 2359304 | tf_op jit(solution)/shard_map/ppermute | solution.py:829
  32.0 0.9 copy-start.1
  32.9 28.0 %copy-start = (bf16[1024,768]{1,0:T(8,128)(2,1)S(1)}, bf16[1024,768]{1,0:T(8,128)(2,1)}, u32[]{:S(2)}) copy-start(bf16[1024,768]{1,0:T(8,128)(2,1)} %param.16) | copy-start | bytes 4718596
  58.6 4.4 %collective-permute-start.1 = (bf16[512,768]{1,0:T(8,128)(2,1)}, bf16[512,768]{1,0:T(8,128)(2,1)S(1)}, u32[]{:S(2)}, u32[]{:S(2)}) collective-permute-start(bf16[512,768]{1,0:T(8,128)(2,1)} %get-tuple-element.79), channel_id=1, source_target_pairs={{0,16},{1,17},{2,18},{3,19},{4,20},{5,21},{6,22},{7,23},{8,24},{9,... | collective-permute-start | bytes 2359304 | tf_op jit(solution)/shard_map/ppermute | solution.py:829
  62.9 0.9 copy-start.2
  72.7 46.4 %collective-permute-start.2 = (bf16[512,768]{1,0:T(8,128)(2,1)}, bf16[512,768]{1,0:T(8,128)(2,1)S(1)}, u32[]{:S(2)}, u32[]{:S(2)}) collective-permute-start(bf16[512,768]{1,0:T(8,128)(2,1)} %get-tuple-element.97), channel_id=1, source_target_pairs={{16,0},{17,1},{18,2},{19,3},{20,4},{21,5},{22,6},{23,7},{24,8},{25... | collective-permute-start | bytes 2359304 | tf_op jit(solution)/shard_map/ppermute | solution.py:829
  119.1 0.9 copy-start.6
  146.9 4.4 %collective-permute-start.3 = (bf16[512,768]{1,0:T(8,128)(2,1)}, bf16[512,768]{1,0:T(8,128)(2,1)S(1)}, u32[]{:S(2)}, u32[]{:S(2)}) collective-permute-start(bf16[512,768]{1,0:T(8,128)(2,1)} %get-tuple-element.103), channel_id=1, source_target_pairs={{16,0},{17,1},{18,2},{19,3},{20,4},{21,5},{22,6},{23,7},{24,8},{25... | collective-permute-start | bytes 2359304 | tf_op jit(solution)/shard_map/ppermute | solution.py:829
  151.3 0.9 copy-start.5
  306.1 9.5 %copy-start.8 = (f32[1,192]{1,0:T(1,128)}, f32[1,192]{1,0:T(1,128)S(1)}, u32[]{:S(2)}) copy-start(f32[1,192]{1,0:T(1,128)S(1)} %get-tuple-element.160) | copy-start | bytes 2308
  306.1 3.0 copy-start.3
  309.1 1.7 copy-start.4
  310.8 1.3 copy-start.7

commit v3 on v2

--- a/solution.py
+++ b/solution.py
@@ -40,66 +40,91 @@
     return jnp.where(v >= 0, 1.0 - tail, tail), bell * 0.3989422804014327
 
 
-class Copies:
-    def __init__(self, sems):
-        self.sems, self.copies = sems, []
-
-    def start(self, src, dst):
-        copy = pltpu.make_async_copy(src, dst, self.sems.at[len(self.copies)])
-        copy.start()
-        self.copies.append(copy)
-        return copy
-
-    def wait(self):
-        for copy in self.copies:
-            copy.wait()
-
-
-def forward_kernel(moment, micros, n_alias, *refs):
+def forward_kernel(micros, *refs):
     (
-        lengths, tokens_h, received_h, attn_gain, attn_shift, qkv_bias, out_bias, mlp_gain, mlp_shift,
-        up_bias, down_bias, cosine, sine, qkv_h, out_h, up_h, down_h,
-    ) = refs[:17]
-    (
-        y_send_h, y_h, attn_in_h, mlp_in_h, queries_h, keys_h, values_h, probs_h, context_h, hidden_h, slope_h,
+        lengths, tokens_h, attn_gain, attn_shift, qkv_bias, out_bias, mlp_gain, mlp_shift, up_bias, down_bias,
+        cosine, sine, qkv_h, out_h, up_h, down_h,
+        y_h, inputs_h, attn_in_h, mlp_in_h, queries_h, keys_h, values_h, probs_h, context_h, hidden_h, slope_h,
         qkv_w, out_w, up_w, down_w, x, attn_in, mlp_in, attn_in_t, mlp_in_t, heads_t, context_t, hidden_t, slope,
-        bias, total, probs, y, in_sems, out_sems, probs_sems,
-    ) = refs[17 + n_alias :]
+        bias, total, probs, y, in_sems, out_sems, probs_sems, send_sems, recv_sems,
+    ) = refs
     section = lax.axis_index("section")
-    micro = moment - section
-    rows, width = x.shape
+    rows, width = attn_in.shape
     hidden_width = up_w.shape[1]
     half = rows // 2
-
-    @pl.when((micro >= 0) & (micro < micros))
+    other = {"section": 1 - section}
+
+    barrier = pltpu.get_barrier_semaphore()
+    pl.semaphore_signal(barrier, inc=1, device_id=other, device_id_type=pl.DeviceIdType.MESH)
+    loads = [
+        pltpu.make_async_copy(src, dst, in_sems.at[i])
+        for i, (src, dst) in enumerate(
+            ((tokens_h, x), (qkv_h, qkv_w), (out_h, out_w), (up_h, up_w), (down_h, down_w))
+        )
+    ]
+
+    @pl.when(section == 0)
     def _():
-        loads = [
-            pltpu.make_async_copy(src, dst, in_sems.at[i])
-            for i, (src, dst) in enumerate(((qkv_h, qkv_w), (out_h, out_w), (up_h, up_w), (down_h, down_w)))
+        loads[0].start()
+
+    loads[1].start()
+    probs[:, half:, :half] = jnp.zeros((probs.shape[0], half, half), BF16)
+    cos_rows, sin_rows = cosine[...], sine[...]
+
+    def hand_over(micro):
+        return pltpu.make_async_remote_copy(
+            src_ref=y.at[micro],
+            dst_ref=x.at[micro],
+            send_sem=send_sems.at[micro],
+            recv_sem=recv_sems.at[micro],
+            device_id=other,
+            device_id_type=pl.DeviceIdType.MESH,
+        )
+
+    def stores(micro):
+        pairs = [
+            (x.at[micro], inputs_h.at[micro]),
+            (attn_in_t, attn_in_h.at[micro]),
+            (mlp_in_t, mlp_in_h.at[micro]),
+            (heads_t.at[0:width], queries_h.at[micro]),
+            (heads_t.at[width : 2 * width], keys_h.at[micro]),
+            (heads_t.at[2 * width :], values_h.at[micro]),
+            (context_t, context_h.at[micro]),
+            (y.at[micro], y_h.at[micro]),
         ]
-        own = pltpu.make_async_copy(tokens_h.at[micro], x, in_sems.at[4])
-        passed = pltpu.make_async_copy(received_h, x, in_sems.at[4])
-
-        @pl.when(section == 0)
-        def _():
-            own.start()
-
-        @pl.when(section != 0)
-        def _():
-            passed.start()
-
-        loads[0].start()
-        stores = Copies(out_sems)
+        for start in range(0, hidden_width, FF_TILE):
+            part = slice(start, start + FF_TILE)
+            pairs.append((hidden_t.at[part], hidden_h.at[micro, part]))
+            pairs.append((slope.at[:, part], slope_h.at[micro, :, part]))
+        return [pltpu.make_async_copy(src, dst, out_sems.at[i]) for i, (src, dst) in enumerate(pairs)]
+
+    pl.semaphore_wait(barrier, 1)
+
+    def sentence(micro, carry):
+        store = stores(micro)
+
+        @pl.when((section == 0) & (micro == 0))
+        def _():
+            loads[0].wait()
+
+        @pl.when(section == 1)
+        def _():
+            hand_over(micro).wait_recv()
+
+        store[0].start()
         length = lengths[micro]
         key_ids = lax.broadcasted_iota(jnp.int32, (rows, rows), 0)
         query_ids = lax.broadcasted_iota(jnp.int32, (rows, rows), 1)
         bias[...] = jnp.where((key_ids <= query_ids) & (key_ids < length), 0.0, MASKED)
-        probs[:, half:, :half] = jnp.zeros((probs.shape[0], half, half), BF16)
-        own.wait()
+
+        @pl.when(micro > 0)
+        def _():
+            for copy in stores(micro - 1):
+                copy.wait()
 
         for start in range(0, rows, ROW_CHUNK):
             part = slice(start, start + ROW_CHUNK)
-            block = x[part, :].astype(F32)
+            block = x[micro, part, :].astype(F32)
             centred = block - jnp.mean(block, axis=-1, keepdims=True)
             unit = centred * lax.rsqrt(jnp.mean(centred * centred, axis=-1, keepdims=True) + EPSILON)
             attn = (unit * attn_gain[...].astype(F32) + attn_shift[...].astype(F32)).astype(BF16)
@@ -108,13 +133,15 @@
             mlp_in[part, :] = mlp
             attn_in_t[:, part] = attn.T
             mlp_in_t[:, part] = mlp.T
-        loads[0].wait()
-        for load in loads[1:]:
-            load.start()
-        stores.start(attn_in_t, attn_in_h.at[micro])
-        stores.start(mlp_in_t, mlp_in_h.at[micro])
-
-        cos_rows, sin_rows = cosine[...], sine[...]
+        store[1].start()
+        store[2].start()
+
+        @pl.when(micro == 0)
+        def _():
+            loads[1].wait()
+            for load in loads[2:]:
+                load.start()
+
         for start in range(0, 3 * width, QKV_TILE):
             part = slice(start, start + QKV_TILE)
             projected = jnp.dot(attn_in[...], qkv_w[:, part], preferred_element_type=F32)
@@ -132,9 +159,8 @@
                     ],
                     axis=0,
                 ).astype(BF16)
-        stores.start(heads_t.at[0:width], queries_h.at[micro])
-        stores.start(heads_t.at[width : 2 * width], keys_h.at[micro])
-        stores.start(heads_t.at[2 * width :], values_h.at[micro])
+        for copy in store[3:6]:
+            copy.start()
 
         def softmax(scores):
             raised = jnp.exp(scores - jnp.max(scores, axis=0, keepdims=True))
@@ -171,15 +197,16 @@
             return carry
 
         lax.fori_loop(0, HEADS // 2, attend_pair, 0)
-        for head in range(HEADS - 4, HEADS):
-            probs_copy(head, head % 4).wait()
-        stores.start(context_t, context_h.at[micro])
-
-        for load in loads[1:]:
-            load.wait()
+        store[6].start()
+
+        @pl.when(micro == 0)
+        def _():
+            for load in loads[2:]:
+                load.wait()
+
         total[...] = (
             dims_dot(context_t[...], out_w[...], 0, 0)
-            + x[...].astype(F32)
+            + x[micro].astype(F32)
             + (out_bias[...].astype(F32) + down_bias[...].astype(F32))
         )
         for start in range(0, hidden_width, FF_TILE):
@@ -190,16 +217,32 @@
             hidden = (up * share).astype(BF16)
             slope[:, part] = (share + up * density).astype(BF16)
             hidden_t[part, :] = hidden.T
-            stores.start(hidden_t.at[part], hidden_h.at[micro, part])
-            stores.start(slope.at[:, part], slope_h.at[micro, :, part])
+            tile = start // FF_TILE
+            store[8 + 2 * tile].start()
+            store[9 + 2 * tile].start()
             total[...] += jnp.dot(hidden, down_w[part, :], preferred_element_type=F32)
-        y[...] = total[...].astype(BF16)
-        stores.start(y, y_send_h)
-        stores.start(y, y_h.at[micro])
-        stores.wait()
-
-
-def forward_call(moment, lengths, tokens, received, weights, tables, stash):
+        y[micro] = total[...].astype(BF16)
+
+        @pl.when(section == 0)
+        def _():
+            hand_over(micro).start()
+
+        store[7].start()
+        for head in range(HEADS - 4, HEADS):
+            probs_copy(head, head % 4).wait()
+        return carry
+
+    lax.fori_loop(0, micros, sentence, 0)
+    for copy in stores(micros - 1):
+        copy.wait()
+
+    @pl.when(section == 0)
+    def _():
+        for micro in range(micros):
+            hand_over(micro).wait_send()
+
+
+def forward_call(lengths, tokens, weights, tables):
     (
         attn_gain, attn_shift, qkv_weight, qkv_bias, out_weight, out_bias, mlp_gain, mlp_shift, up_weight, up_bias,
         down_weight, down_bias,
@@ -208,124 +251,165 @@
     hidden_width = up_weight.shape[1]
     wide, tall = (micros, rows, width), (micros, width, rows)
     shapes = [
-        (rows, width), wide, tall, tall, tall, tall, tall, (micros, HEADS, rows, rows), tall,
-        (micros, hidden_width, rows), (micros, rows, hidden_width),
+        wide, wide, tall, tall, tall, tall, tall, (micros, HEADS, rows, rows), tall, (micros, hidden_width, rows),
+        (micros, rows, hidden_width),
     ]
-    kept = () if stash is None else tuple(stash)
     buffers = [
-        qkv_weight.shape, out_weight.shape, up_weight.shape, down_weight.shape, (rows, width), (rows, width),
-        (rows, width), (width, rows), (width, rows), (3 * width, rows), (width, rows), (hidden_width, rows),
-        (rows, hidden_width),
+        qkv_weight.shape, out_weight.shape, up_weight.shape, down_weight.shape, wide, (rows, width), (rows, width),
+        (width, rows), (width, rows), (3 * width, rows), (width, rows), (hidden_width, rows), (rows, hidden_width),
     ]
-    outs = pl.pallas_call(
-        functools.partial(forward_kernel, moment, micros, len(kept)),
+    return pl.pallas_call(
+        functools.partial(forward_kernel, micros),
         out_shape=[jax.ShapeDtypeStruct(shape, BF16) for shape in shapes],
-        in_specs=[SMEM, ANY, ANY] + [VMEM] * 10 + [ANY] * (4 + len(kept)),
+        in_specs=[SMEM, ANY] + [VMEM] * 10 + [ANY] * 4,
         out_specs=[ANY] * len(shapes),
         scratch_shapes=[pltpu.VMEM(shape, BF16) for shape in buffers]
         + [
             pltpu.VMEM((rows, rows), F32),
             pltpu.VMEM((rows, width), F32),
             pltpu.VMEM((4, rows, rows), BF16),
-            pltpu.VMEM((rows, width), BF16),
+            pltpu.VMEM(wide, BF16),
             pltpu.SemaphoreType.DMA((5,)),
             pltpu.SemaphoreType.DMA((8 + 2 * (hidden_width // FF_TILE),)),
             pltpu.SemaphoreType.DMA((4,)),
+            pltpu.SemaphoreType.DMA((micros,)),
+            pltpu.SemaphoreType.DMA((micros,)),
         ],
-        input_output_aliases={17 + i: 1 + i for i in range(len(kept))},
-        compiler_params=pltpu.CompilerParams(vmem_limit_bytes=56 << 20),
+        compiler_params=pltpu.CompilerParams(collective_id=1, has_side_effects=True, vmem_limit_bytes=58 << 20),
         cost_estimate=pl.CostEstimate(
-            flops=2 * rows * width * (4 * width + 2 * hidden_width) + 4 * rows * rows * width,
-            bytes_accessed=40 << 20,
-            transcendentals=rows * hidden_width,
+            flops=micros * (2 * rows * width * (4 * width + 2 * hidden_width) + 4 * rows * rows * width),
+            bytes_accessed=80 << 20,
+            transcendentals=micros * rows * hidden_width,
         ),
         name="layer_forward",
     )(
-        lengths, tokens, received, attn_gain, attn_shift, qkv_bias, out_bias, mlp_gain, mlp_shift, up_bias,
-        down_bias, *tables, qkv_weight, out_weight, up_weight, down_weight, *kept,
+        lengths, tokens, attn_gain, attn_shift, qkv_bias, out_bias, mlp_gain, mlp_shift, up_bias, down_bias,
+        *tables, qkv_weight, out_weight, up_weight, down_weight,
     )
-    return outs[0], outs[1:]
-
-
-def backward_kernel(moment, micros, n_alias, *refs):
-    n_in = 17 + micros
-    lengths, cotangent_h, received_h, tokens_h = refs[:4]
-    passed_h = refs[4 : 4 + micros]
+
+
+def backward_kernel(micros, *refs):
     (
-        attn_gain, mlp_gain, cosine, sine, qkv_h, out_h, up_h, down_h, queries_h, keys_h, values_h, probs_h,
-        context_h, slope_h,
-    ) = refs[4 + micros : 18 + micros]
-    (
-        send_h, grad_in_h, grad_heads_h, grad_up_h, grad_out_h, vectors_h,
+        lengths, cotangent_h, inputs_h, attn_gain, mlp_gain, cosine, sine, qkv_h, out_h, up_h, down_h,
+        queries_h, keys_h, values_h, probs_h, context_h, slope_h,
+        grad_in_h, grad_heads_h, grad_up_h, grad_out_h, vectors_h,
         qkv_w, out_w, up_w, down_w, queries, keys, values, context, slope, probs, grad_out, x, grad_context,
-        grad_up, grad_heads, grad_low, grad_mlp, grad_in, column_sums, vectors, in_sems, out_sems, probs_sems,
-    ) = refs[18 + micros + n_alias :]
+        grad_up, grad_heads, grad_low, grad_mlp, grad_in, column_sums, vectors,
+        in_sems, stash_sems, out_sems, probs_sems, send_sems, recv_sems,
+    ) = refs
     section = lax.axis_index("section")
-    last = lax.axis_size("section") - 1
-    micro = moment - (last - section)
     rows, width = x.shape
     hidden_width = up_w.shape[1]
     half = rows // 2
-
-    @pl.when((micro >= 0) & (micro < micros))
+    other = {"section": 1 - section}
+
+    barrier = pltpu.get_barrier_semaphore()
+    pl.semaphore_signal(barrier, inc=1, device_id=other, device_id_type=pl.DeviceIdType.MESH)
+    loads = [
+        pltpu.make_async_copy(src, dst, in_sems.at[i])
+        for i, (src, dst) in enumerate(
+            ((cotangent_h, grad_out), (out_h, out_w), (down_h, down_w), (up_h, up_w), (qkv_h, qkv_w))
+        )
+    ]
+
+    def stash_loads(micro):
+        pairs = (
+            (slope_h, slope), (values_h, values), (context_h, context), (queries_h, queries), (keys_h, keys),
+            (inputs_h, x),
+        )
+        return [
+            pltpu.make_async_copy(src.at[micro], dst, stash_sems.at[i]) for i, (src, dst) in enumerate(pairs)
+        ]
+
+    @pl.when(section == 1)
     def _():
-        loads = [
-            pltpu.make_async_copy(src, dst, in_sems.at[i])
-            for i, (src, dst) in enumerate(
-                (
-                    (out_h, out_w), (down_h, down_w), (slope_h.at[micro], slope), (up_h, up_w),
-                    (values_h.at[micro], values), (context_h.at[micro], context), (queries_h.at[micro], queries),
-                    (keys_h.at[micro], keys), (qkv_h, qkv_w),
-                )
-            )
+        loads[0].start()
+
+    for load in loads[1:3]:
+        load.start()
+    stash_loads(0)[0].start()
+    loads[3].start()
+    for load in stash_loads(0)[1:]:
+        load.start()
+    loads[4].start()
+    cos_rows, sin_rows = cosine[...], sine[...]
+    attn_column = jnp.broadcast_to(attn_gain[...].astype(F32), (8, width)).T[:, 0:1]
+    mlp_column = jnp.broadcast_to(mlp_gain[...].astype(F32), (8, width)).T[:, 0:1]
+
+    def hand_over(micro):
+        return pltpu.make_async_remote_copy(
+            src_ref=grad_low.at[micro],
+            dst_ref=grad_out.at[micro],
+            send_sem=send_sems.at[micro],
+            recv_sem=recv_sems.at[micro],
+            device_id=other,
+            device_id_type=pl.DeviceIdType.MESH,
+        )
+
+    def stores(micro):
+        pairs = [
+            (grad_out.at[micro], grad_out_h.at[micro]),
+            (grad_heads, grad_heads_h.at[micro]),
+            (grad_in, grad_in_h.at[micro]),
+            (vectors, vectors_h.at[micro]),
         ]
-        own = pltpu.make_async_copy(cotangent_h.at[micro], grad_out, in_sems.at[9])
-        passed = pltpu.make_async_copy(received_h, grad_out, in_sems.at[9])
-        block = pltpu.make_async_copy(tokens_h.at[micro], x, in_sems.at[10])
-
-        @pl.when(section == last)
-        def _():
-            own.start()
-
-        @pl.when(section != last)
-        def _():
-            passed.start()
-
-        for load in loads[:4]:
-            load.start()
+        for start in range(0, hidden_width, FF_TILE):
+            part = slice(start, start + FF_TILE)
+            pairs.append((grad_up.at[:, part], grad_up_h.at[micro, :, part]))
+        return [pltpu.make_async_copy(src, dst, out_sems.at[i]) for i, (src, dst) in enumerate(pairs)]
+
+    pl.semaphore_wait(barrier, 1)
+
+    def sentence(micro, carry):
+        store = stores(micro)
+        stash = stash_loads(micro)
+        upcoming = stash_loads(micro + 1)
+
+        def probs_copy(head, slot):
+            return pltpu.make_async_copy(probs_h.at[micro, head], probs.at[slot], probs_sems.at[slot])
+
+        for head in range(2):
+            probs_copy(head, head).start()
+
+        @pl.when((section == 1) & (micro == 0))
+        def _():
+            loads[0].wait()
 
         @pl.when(section == 0)
         def _():
-            block.start()
-
-        for one, source in enumerate(passed_h):
-
-            @pl.when((section != 0) & (micro == one))
-            def _():
-                pltpu.make_async_copy(source, x, in_sems.at[10]).start()
-
-        stores = Copies(out_sems)
-        length = lengths[micro]
+            hand_over(micro).wait_recv()
+
         row_ids = lax.broadcasted_iota(jnp.int32, (rows, 1), 0)
-        own.wait()
-        grad_wide = jnp.where(row_ids < length, grad_out[...].astype(F32), 0.0)
-        grad_out[...] = grad_wide.astype(BF16)
+        grad_wide = jnp.where(row_ids < lengths[micro], grad_out[micro].astype(F32), 0.0)
+        grad_out[micro] = grad_wide.astype(BF16)
+
+        @pl.when(micro > 0)
+        def _():
+            for copy in stores(micro - 1):
+                copy.wait()
+
         vectors[...] = jnp.zeros_like(vectors)
         vectors[7:8, :] = jnp.sum(grad_wide, axis=0, keepdims=True)
-        stores.start(grad_out, grad_out_h.at[micro])
-        loads[0].wait()
-        for load in loads[4:]:
-            load.start()
-        grad_context[...] = dims_dot(out_w[...], grad_out[...], 1, 1).astype(BF16)
-
-        for load in loads[1:4]:
-            load.wait()
+        store[0].start()
+
+        @pl.when(micro == 0)
+        def _():
+            loads[1].wait()
+
+        grad_context[...] = dims_dot(out_w[...], grad_out[micro], 1, 1).astype(BF16)
+
+        @pl.when(micro == 0)
+        def _():
+            loads[2].wait()
+            loads[3].wait()
+
+        stash[0].wait()
         for start in range(0, hidden_width, FF_TILE):
             part = slice(start, start + FF_TILE)
-            grad_hidden = dims_dot(grad_out[...], down_w[part, :], 1, 1)
+            grad_hidden = dims_dot(grad_out[micro], down_w[part, :], 1, 1)
             grad_pre = (grad_hidden * slope[:, part].astype(F32)).astype(BF16)
             grad_up[:, part] = grad_pre
-            stores.start(grad_up.at[:, part], grad_up_h.at[micro, :, part])
+            store[4 + start // FF_TILE].start()
             sums = jnp.sum(grad_pre.astype(F32), axis=0, keepdims=True)
             for at in range(0, FF_TILE, 128):
                 row, column = divmod(start + at, width)
@@ -336,9 +420,12 @@
             else:
                 grad_mlp[...] += back
 
-        for load in loads[4:8]:
+        @pl.when(micro < micros - 1)
+        def _():
+            upcoming[0].start()
+
+        for load in stash[1:5]:
             load.wait()
-        cos_rows, sin_rows = cosine[...], sine[...]
 
         def turn_back(grad):
             low, high = grad[:HALF], grad[HALF:ROTARY]
@@ -373,12 +460,6 @@
             grad_heads[pl.ds(width + at, HEAD_DIM), :] = turn_back(grad_key * SCALE).astype(BF16)
             grad_heads[pl.ds(2 * width + at, HEAD_DIM), :] = grad_value.astype(BF16)
 
-        def probs_copy(head, slot):
-            return pltpu.make_async_copy(probs_h.at[micro, head], probs.at[slot], probs_sems.at[slot])
-
-        for head in range(2):
-            probs_copy(head, head).start()
-
         def attend_pair(pair, carry):
             first_slot = 2 * lax.rem(pair, 2)
 
@@ -394,12 +475,18 @@
             return carry
 
         lax.fori_loop(0, HEADS // 2, attend_pair, 0)
-        stores.start(grad_heads, grad_heads_h.at[micro])
-
-        loads[8].wait()
-        block.wait()
-        attn_column = jnp.broadcast_to(attn_gain[...].astype(F32), (8, width)).T[:, 0:1]
-        mlp_column = jnp.broadcast_to(mlp_gain[...].astype(F32), (8, width)).T[:, 0:1]
+        store[1].start()
+
+        @pl.when(micro < micros - 1)
+        def _():
+            for load in upcoming[1:5]:
+                load.start()
+
+        @pl.when(micro == 0)
+        def _():
+            loads[4].wait()
+
+        stash[5].wait()
         column_sums[...] = jnp.zeros_like(column_sums)
 
         def norm_chunk(index, carry):
@@ -416,9 +503,9 @@
                 - jnp.mean(grad_unit, axis=0, keepdims=True)
                 - unit * jnp.mean(grad_unit * unit, axis=0, keepdims=True)
             )
-            exact = through.T + grad_out[part, :].astype(F32)
+            exact = through.T + grad_out[micro, part, :].astype(F32)
             low = exact.astype(BF16)
-            grad_low[part, :] = low
+            grad_low[micro, part, :] = low
             grad_in[part, :] = jnp.where(section == 0, exact, low.astype(F32))
             column_sums[0] += grad_attn_in * unit
             column_sums[1] += grad_attn_in
@@ -427,8 +514,16 @@
             return carry
 
         lax.fori_loop(0, rows // ROW_CHUNK, norm_chunk, 0)
-        stores.start(grad_low, send_h)
-        stores.start(grad_in, grad_in_h.at[micro])
+
+        @pl.when(section == 1)
+        def _():
+            hand_over(micro).start()
+
+        @pl.when(micro < micros - 1)
+        def _():
+            upcoming[5].start()
+
+        store[2].start()
         columns = [jnp.sum(column_sums[i], axis=1, keepdims=True) for i in range(4)]
         for start in range(0, 3 * width, width):
             columns.append(jnp.sum(grad_heads[start : start + width, :].astype(F32), axis=1, keepdims=True))
@@ -437,31 +532,37 @@
         for lane, column in enumerate(columns):
             gathered = jnp.where(lanes == lane, column, gathered)
         vectors[0:7, :] = gathered.T[0:7, :]
-        stores.start(vectors, vectors_h.at[micro])
-        stores.wait()
-
-
-def backward_call(moment, lengths, cotangent, received, tokens, passed, weights, tables, stash, kept):
+        store[3].start()
+        return carry
+
+    lax.fori_loop(0, micros, sentence, 0)
+    for copy in stores(micros - 1):
+        copy.wait()
+
+    @pl.when(section == 1)
+    def _():
+        for micro in range(micros):
+            hand_over(micro).wait_send()
+
+
+def backward_call(lengths, cotangent, weights, tables, stash):
     attn_gain, _, qkv_weight, _, out_weight, _, mlp_gain, _, up_weight, _, down_weight, _ = weights
-    _, _, _, queries, keys, values, probs, context, _, slope = stash
-    micros, rows, width = tokens.shape
+    _, inputs, _, _, queries, keys, values, probs, context, _, slope = stash
+    micros, rows, width = cotangent.shape
     hidden_width = up_weight.shape[1]
     vector_rows = 16
-    kept = () if kept is None else tuple(kept)
+    wide, tall = (micros, rows, width), (width, rows)
     outs = [
-        jax.ShapeDtypeStruct((rows, width), BF16),
-        jax.ShapeDtypeStruct((micros, rows, width), F32),
+        jax.ShapeDtypeStruct(wide, F32),
         jax.ShapeDtypeStruct((micros, 3 * width, rows), BF16),
         jax.ShapeDtypeStruct((micros, rows, hidden_width), BF16),
-        jax.ShapeDtypeStruct((micros, rows, width), BF16),
+        jax.ShapeDtypeStruct(wide, BF16),
         jax.ShapeDtypeStruct((micros, vector_rows, width), F32),
     ]
-    tall = (width, rows)
-    n_in = 18 + micros
-    results = pl.pallas_call(
-        functools.partial(backward_kernel, moment, micros, len(kept)),
+    return pl.pallas_call(
+        functools.partial(backward_kernel, micros),
         out_shape=outs,
-        in_specs=[SMEM] + [ANY] * (3 + micros) + [VMEM] * 4 + [ANY] * (10 + len(kept)),
+        in_specs=[SMEM] + [ANY] * 2 + [VMEM] * 4 + [ANY] * 10,
         out_specs=[ANY] * len(outs),
         scratch_shapes=[
             pltpu.VMEM(qkv_weight.shape, BF16),
@@ -474,33 +575,34 @@
             pltpu.VMEM(tall, BF16),
             pltpu.VMEM((rows, hidden_width), BF16),
             pltpu.VMEM((4, rows, rows), BF16),
-            pltpu.VMEM((rows, width), BF16),
+            pltpu.VMEM(wide, BF16),
             pltpu.VMEM((rows, width), BF16),
             pltpu.VMEM(tall, BF16),
             pltpu.VMEM((rows, hidden_width), BF16),
             pltpu.VMEM((3 * width, rows), BF16),
-            pltpu.VMEM((rows, width), BF16),
+            pltpu.VMEM(wide, BF16),
             pltpu.VMEM(tall, F32),
             pltpu.VMEM((rows, width), F32),
             pltpu.VMEM((4, width, 128), F32),
             pltpu.VMEM((vector_rows, width), F32),
-            pltpu.SemaphoreType.DMA((11,)),
-            pltpu.SemaphoreType.DMA((5 + hidden_width // FF_TILE,)),
+            pltpu.SemaphoreType.DMA((5,)),
+            pltpu.SemaphoreType.DMA((6,)),
+            pltpu.SemaphoreType.DMA((4 + hidden_width // FF_TILE,)),
             pltpu.SemaphoreType.DMA((4,)),
+            pltpu.SemaphoreType.DMA((micros,)),
+            pltpu.SemaphoreType.DMA((micros,)),
         ],
-        input_output_aliases={n_in + i: 1 + i for i in range(len(kept))},
-        compiler_params=pltpu.CompilerParams(vmem_limit_bytes=58 << 20),
+        compiler_params=pltpu.CompilerParams(collective_id=2, has_side_effects=True, vmem_limit_bytes=58 << 20),
         cost_estimate=pl.CostEstimate(
-            flops=2 * rows * width * (4 * width + 2 * hidden_width) + 8 * rows * rows * width,
-            bytes_accessed=40 << 20,
+            flops=micros * (2 * rows * width * (4 * width + 2 * hidden_width) + 8 * rows * rows * width),
+            bytes_accessed=80 << 20,
             transcendentals=0,
         ),
         name="layer_backward",
     )(
-        lengths, cotangent, received, tokens, *passed, attn_gain, mlp_gain, *tables, qkv_weight, out_weight,
-        up_weight, down_weight, queries, keys, values, probs, context, slope, *kept,
+        lengths, cotangent, inputs, attn_gain, mlp_gain, *tables, qkv_weight, out_weight, up_weight, down_weight,
+        queries, keys, values, probs, context, slope,
     )
-    return results[0], results[1:]
 
 
 def partner(axis, bit):
@@ -753,7 +855,7 @@
 
 
 def reduce_call(stash, kept):
-    _, attn_in, mlp_in, _, _, _, _, context, hidden, _ = stash
+    _, _, attn_in, mlp_in, _, _, _, _, context, hidden, _ = stash
     _, grad_heads, grad_up, grad_out, vectors = kept
     micros, width, rows = attn_in.shape
     hidden_width = hidden.shape[1]
@@ -823,10 +925,66 @@
     return scattered, sums
 
 
-def shifted(value, axis, by):
-    size = lax.axis_size(axis)
-    pairs = [(i, i + by) for i in range(size) if 0 <= i + by < size]
-    return lax.ppermute(value, axis, pairs)
+def finish_kernel(grad_scale, *refs):
+    vectors = refs[0]
+    sources = refs[1:7]
+    targets = refs[7:13]
+    vector_outs = refs[13:21]
+    held, wide = refs[21:27], refs[27:31]
+    in_sems, out_sems = refs[31:]
+    ready = (*held[:2], *wide)
+    loads = [pltpu.make_async_copy(src, dst, in_sems.at[i]) for i, (src, dst) in enumerate(zip(sources, held))]
+    stores = [pltpu.make_async_copy(src, dst, out_sems.at[i]) for i, (src, dst) in enumerate(zip(ready, targets))]
+    for load in loads:
+        load.start()
+    devices = lax.axis_size("dp")
+    mine = lax.axis_index("dp")
+    width = vectors.shape[1]
+    first_rows = (0, 1, 4, 7, 2, 3, 8, 7)
+    for device in range(devices):
+
+        @pl.when(mine == device)
+        def _():
+            for out, first in zip(vector_outs, first_rows):
+                at, size, filled = device * out.shape[1], out.shape[1], 0
+                while filled < size:
+                    row, column = divmod(at + filled, width)
+                    count = min(size - filled, width - column)
+                    piece = vectors[first + row : first + row + 1, column : column + count]
+                    out[:, filled : filled + count] = piece * grad_scale
+                    filled += count
+
+    for i, (load, store) in enumerate(zip(loads, stores)):
+        load.wait()
+        if i >= 2:
+            wide[i - 2][...] = held[i][...].astype(F32) * grad_scale
+        store.start()
+    for store in stores:
+        store.wait()
+
+
+def finish_call(grad_scale, shares, vectors, outputs, grad_in, hidden_width):
+    width = vectors.shape[1]
+    devices = lax.axis_size("dp")
+    sizes = [width, width, 3 * width, width, width, width, hidden_width, width]
+    matrices = [jax.ShapeDtypeStruct(share.shape, F32) for share in shares]
+    results = pl.pallas_call(
+        functools.partial(finish_kernel, grad_scale),
+        out_shape=[
+            jax.ShapeDtypeStruct(outputs.shape, BF16),
+            jax.ShapeDtypeStruct(grad_in.shape, F32),
+            *matrices,
+            *[jax.ShapeDtypeStruct((1, size // devices), F32) for size in sizes],
+        ],
+        in_specs=[VMEM] + [ANY] * 6,
+        out_specs=[ANY] * 6 + [VMEM] * 8,
+        scratch_shapes=[pltpu.VMEM(array.shape, array.dtype) for array in (outputs, grad_in, *shares)]
+        + [pltpu.VMEM(share.shape, F32) for share in shares]
+        + [pltpu.SemaphoreType.DMA((6,)), pltpu.SemaphoreType.DMA((6,))],
+        compiler_params=pltpu.CompilerParams(vmem_limit_bytes=60 << 20),
+        name="finish",
+    )(vectors, outputs, grad_in, *shares)
+    return results[:2], results[2:6], results[6:]
 
 
 def rotary_tables(seq_len):
@@ -847,7 +1005,7 @@
 
 
 def local_totals(stash, kept):
-    _, attn_in, mlp_in, _, _, _, _, context, hidden, _ = stash
+    _, _, attn_in, mlp_in, _, _, _, _, context, hidden, _ = stash
     _, grad_heads, grad_up, grad_out, vectors = kept
     vector_sums = jnp.sum(vectors, axis=0)
     groups = hidden.shape[1] // attn_in.shape[1]
@@ -872,45 +1030,22 @@
     micros = lengths.shape[0]
     width = tokens.shape[1]
     rows = tokens.shape[0] // micros
-    sections = lax.axis_size("section")
-    inputs = tokens.reshape(micros, rows, width)
-    cotans = cotangent.reshape(micros, rows, width)
     tables = rotary_tables(rows)
-
-    stash, received, passed = None, inputs[0], []
-    for moment in range(micros + sections - 1):
-        sent, stash = forward_call(moment, lengths, inputs, received, weights, tables, stash)
-        if moment < micros:
-            received = shifted(sent, "section", 1)
-            passed.append(received)
-
-    kept, received = None, cotans[0]
-    for moment in range(micros + sections - 1):
-        sent, kept = backward_call(
-            moment, lengths, cotans, received, inputs, passed, weights, tables, stash, kept
-        )
-        if moment < micros:
-            received = shifted(sent, "section", -1)
-
+    stash = forward_call(lengths, tokens.reshape(micros, rows, width), weights, tables)
+    kept = backward_call(lengths, cotangent.reshape(micros, rows, width), weights, tables, stash)
     grad_scale = float(tokens.shape[0] * lax.axis_size("dp") * lax.axis_size("replica")) ** (-0.5)
     if in_pieces(width):
-        matrices, vectors = reduce_call(stash, kept)
-        mine = lax.axis_index("dp")
-        devices = lax.axis_size("dp")
-
-        def slice_of(first, count):
-            size = count * width // devices
-            return lax.dynamic_slice_in_dim(vectors[first : first + count].reshape(-1), mine * size, size)
-
-        down_bias = slice_of(7, 1)
-        shares = (
-            slice_of(0, 1), slice_of(1, 1), matrices[0], slice_of(4, 3), matrices[1], down_bias, slice_of(2, 1),
-            slice_of(3, 1), matrices[2], slice_of(8, weights[8].shape[1] // width), matrices[3], down_bias,
+        shares, vectors = reduce_call(stash, kept)
+        (outputs, grad_in), matrices, parts = finish_call(
+            grad_scale, shares, vectors, stash[0], kept[0], weights[8].shape[1]
         )
+        qkv, out, up, down = (matrix[None] for matrix in matrices)
+        gain, shift, qkv_bias, out_bias, mlp_gain, mlp_shift, up_bias, down_bias = parts
+        grads = (gain, shift, qkv, qkv_bias, out, out_bias, mlp_gain, mlp_shift, up, up_bias, down, down_bias)
     else:
-        shares = tuple(summed(total) for total in local_totals(stash, kept))
-    scaled = tuple(share.astype(F32)[None] * grad_scale for share in shares)
-    return (stash[0].reshape(1, micros * rows, width), kept[0].reshape(1, micros * rows, width), *scaled)
+        outputs, grad_in = stash[0], kept[0]
+        grads = tuple(summed(total)[None] * grad_scale for total in local_totals(stash, kept))
+    return (outputs.reshape(1, micros * rows, width), grad_in.reshape(1, micros * rows, width), *grads)
 
 
 def solution(mesh):

time: 320 us -> 272 us (0.85)
  waiting for transfers between devices: 51.3 us -> 0 us
  Pallas kernels: 237 us -> 270 us
  local copies, waits for them, and re-layouts: 10.7 us -> 0 us
  other arithmetic: 9.72 us -> 0.77 us
  starting transfers between devices: 6.24 us -> 0 us
    ppermute x4 -> x0, waiting for transfers between devices: 51.3 us -> none  [shifted(): return lax.ppermute(value, axis, pairs)]
    pallas_call x6 -> x3, Pallas kernels: 114 us -> 144 us  [the longest x1 89.7 us: backward_call(): pl.pallas_call(functools.partial(backward_kernel, micros), out_shape=outs...]
    mul x9 -> x0, other arithmetic: 8.96 us -> none  [body(): scaled = tuple((share.astype(F32)[None] * grad_scale for share in shares))]
    ppermute x4 -> x0, starting transfers between devices: 6.24 us -> none  [shifted(): return lax.ppermute(value, axis, pairs)]
    slice x5 -> x0, local copies, waits for them, and re-layouts: 5.41 us -> none  [the longest x3 2.42 us: slice_of(): vectors[first:first + count].reshape(-1)]
    unnamed x19 -> x0, local copies, waits for them, and re-layouts: 4.15 us -> none
  transfers between devices with their start and end apart: 4 -> 0, of which waited for: 4 -> 0; matrix products, arithmetic and copies ran while one was open for 0% -> 0% of each run, Pallas kernels for 0% -> 0%
where the time goes in v3:
time: 272 us; the launch traced here: 271 us
  Pallas kernels  270 us (99%)
    pallas_call x1, Pallas kernels, reduce_call(): pl.pallas_call(functools.partial(reduce_kernel, bits, piece), out_shape=[...  126 us
    pallas_call x1, Pallas kernels, backward_call(): pl.pallas_call(functools.partial(backward_kernel, micros), out_shape=outs...  89.7 us
    pallas_call x1, Pallas kernels, forward_call(): pl.pallas_call(functools.partial(forward_kernel, micros), out_shape=[jax....  45.9 us
    pallas_call x1, Pallas kernels, finish_call(): pl.pallas_call(functools.partial(finish_kernel, grad_scale), out_shape=[j...  8.55 us

profile of v3, /device:TPU:0, one launch (start us, length us, event | category | flops | bytes accessed | tf_op | source)
XLA Modules:
  0.0 271.4 jit_solution(2281012071834178351)
XLA Ops:
  0.7 0.8 fusion
  1.4 45.9 %layer_forward.1 = (bf16[2,512,768]{2,1,0:T(8,128)(2,1)}, bf16[2,512,768]{2,1,0:T(8,128)(2,1)}, bf16[2,768,512]{2,1,0:T(8,128)(2,1)}, bf16[2,768,512]{2,1,0:T(8,...) custom-call(s32[2]{0:T(128)} %refs_0_.3, ...), custom_call_target="tpu_custom_call" | custom-call | flops 16106127360 | bytes 83886080 | tf_op jit(solution)/shard_map/layer_forward/pallas_call | solution.py:261
  47.3 89.7 %layer_backward.1 = (f32[2,512,768]{2,1,0:T(8,128)}, bf16[2,2304,512]{2,1,0:T(8,128)(2,1)}, bf16[2,512,3072]{2,1,0:T(8,128)(2,1)}, bf16[2,512,768]{2,1,0:T(8,128)(2,1)}, f32[2,16,768]{2,1,0:T(8,128)}) custom-call(s32[2]{0:T(128)} %refs_0_.3, bf16[2,512,768]{2,1,0:T(8,128)(2,1)} %bitcast.35, bf16[2,512,768]{2,1,0:T(8,128)(2,1)} %get-tuple-element.53.refs_2_, ...), custom_call_target="tpu_custom_call" | custom-call | flops 17716740096 | bytes 83886080 | tf_op jit(solution)/shard_map/layer_backward/pallas_call | solution.py:562
  137.0 125.7 %weight_gradients.1 = (bf16[2,2,48,2304]{3,2,1,0:T(8,128)(2,1)}, bf16[2,2,48,768]{3,2,1,0:T(8,128)(2,1)}, bf16[2,2,48,3072]{3,2,1,0:T(8,128)(2,1)}, bf16[4,2,2,48,768]{4,3,2,1,0:T(8,128)(2,1)}, f32[16,768]{1,0:T(8,128)}) custom-call(bf16[2,4,192,512]{3,2,1,0:T(8,128)(2,1)} %bitcast.43, bf16[2,4,4,192,512]{4,3,2,1,0:T(8,128)(2,1)} %bitcast.40, ...), custom_call_target="tpu_custom_call" | custom-call | flops 14495514624 | bytes 31457280 | tf_op jit(solution)/shard_map/weight_gradients/pallas_call | solution.py:874
  262.7 8.6 %finish.1 = (bf16[2,512,768]{2,1,0:T(8,128)(2,1)}, f32[2,512,768]{2,1,0:T(8,128)}, f32[192,2304]{1,0:T(8,128)}, f32[192,768]{1,0:T(8,128)}, f32[192,3072]{1,0:T(...) custom-call(f32[16,768]{1,0:T(8,128)} %get-tuple-element.63.refs_0_,, ...), custom_call_target="tpu_custom_call" | custom-call | tf_op jit(solution)/shard_map/finish/pallas_call | solution.py:971
  (1 shorter events, 0.0 us)

commit v4 on v3

--- a/solution.py
+++ b/solution.py
@@ -14,6 +14,8 @@
 EPSILON = 1e-05
 ROTARY_BASE = 10000.0
 MASKED = -1e30
+LOG2_E = 1.4426950408889634
+LOG2_DENSITY = -1.3257480647361593
 SCALE = HEAD_DIM**-0.5
 F32 = jnp.float32
 BF16 = jnp.bfloat16
@@ -21,8 +23,9 @@
 VMEM = pl.BlockSpec(memory_space=pltpu.VMEM)
 SMEM = pl.BlockSpec(memory_space=pltpu.SMEM)
 ROW_CHUNK = 128
+NORM_CHUNK = 256
 QKV_TILE = 256
-FF_TILE = 512
+FF_TILE = 768
 PIECE = 384
 
 
@@ -33,11 +36,9 @@
 
 
 def normal_parts(v):
-    t = 1.0 / (1.0 + (0.3275911 * 0.7071067811865476) * jnp.abs(v))
-    bell = jnp.exp(-0.5 * v * v)
-    series = 0.7107068705 + t * (-0.7265760135 + t * 0.5307027145)
-    tail = t * (0.127414796 + t * (-0.142248368 + t * series)) * bell
-    return jnp.where(v >= 0, 1.0 - tail, tail), bell * 0.3989422804014327
+    scaled = v * 0.7071067811865476
+    bell = jnp.exp2(LOG2_DENSITY - scaled * (scaled * LOG2_E))
+    return 0.5 + 0.5 * lax.erf(scaled), bell
 
 
 def forward_kernel(micros, *refs):
@@ -103,6 +104,12 @@
     def sentence(micro, carry):
         store = stores(micro)
 
+        def settle(first, end):
+            @pl.when(micro > 0)
+            def _():
+                for copy in stores(micro - 1)[first:end]:
+                    copy.wait()
+
         @pl.when((section == 0) & (micro == 0))
         def _():
             loads[0].wait()
@@ -111,17 +118,13 @@
         def _():
             hand_over(micro).wait_recv()
 
-        store[0].start()
         length = lengths[micro]
         key_ids = lax.broadcasted_iota(jnp.int32, (rows, rows), 0)
         query_ids = lax.broadcasted_iota(jnp.int32, (rows, rows), 1)
         bias[...] = jnp.where((key_ids <= query_ids) & (key_ids < length), 0.0, MASKED)
 
-        @pl.when(micro > 0)
-        def _():
-            for copy in stores(micro - 1):
-                copy.wait()
-
+        settle(0, 3)
+        store[0].start()
         for start in range(0, rows, ROW_CHUNK):
             part = slice(start, start + ROW_CHUNK)
             block = x[micro, part, :].astype(F32)
@@ -142,6 +145,7 @@
             for load in loads[2:]:
                 load.start()
 
+        settle(3, 6)
         for start in range(0, 3 * width, QKV_TILE):
             part = slice(start, start + QKV_TILE)
             projected = jnp.dot(attn_in[...], qkv_w[:, part], preferred_element_type=F32)
@@ -196,6 +200,7 @@
                 probs_copy(2 * pair + own_head, first_slot + own_head).start()
             return carry
 
+        settle(6, 7)
         lax.fori_loop(0, HEADS // 2, attend_pair, 0)
         store[6].start()
 
@@ -209,6 +214,7 @@
             + x[micro].astype(F32)
             + (out_bias[...].astype(F32) + down_bias[...].astype(F32))
         )
+        settle(7, len(store))
         for start in range(0, hidden_width, FF_TILE):
             part = slice(start, start + FF_TILE)
             up = jnp.dot(mlp_in[...], up_w[:, part], preferred_element_type=F32)
@@ -365,6 +371,12 @@
         stash = stash_loads(micro)
         upcoming = stash_loads(micro + 1)
 
+        def settle(first, end):
+            @pl.when(micro > 0)
+            def _():
+                for copy in stores(micro - 1)[first:end]:
+                    copy.wait()
+
         def probs_copy(head, slot):
             return pltpu.make_async_copy(probs_h.at[micro, head], probs.at[slot], probs_sems.at[slot])
 
@@ -383,11 +395,8 @@
         grad_wide = jnp.where(row_ids < lengths[micro], grad_out[micro].astype(F32), 0.0)
         grad_out[micro] = grad_wide.astype(BF16)
 
-        @pl.when(micro > 0)
-        def _():
-            for copy in stores(micro - 1):
-                copy.wait()
-
+        settle(0, 1)
+        settle(3, len(store))
         vectors[...] = jnp.zeros_like(vectors)
         vectors[7:8, :] = jnp.sum(grad_wide, axis=0, keepdims=True)
         store[0].start()
@@ -474,6 +483,7 @@
                 attend(2 * pair + own_head, first_slot + own_head)
             return carry
 
+        settle(1, 2)
         lax.fori_loop(0, HEADS // 2, attend_pair, 0)
         store[1].start()
 
@@ -488,9 +498,10 @@
 
         stash[5].wait()
         column_sums[...] = jnp.zeros_like(column_sums)
+        settle(2, 3)
 
         def norm_chunk(index, carry):
-            part = pl.ds(pl.multiple_of(index * ROW_CHUNK, ROW_CHUNK), ROW_CHUNK)
+            part = pl.ds(pl.multiple_of(index * NORM_CHUNK, NORM_CHUNK), NORM_CHUNK)
             grad_attn_in = jnp.dot(qkv_w[...], grad_heads[:, part], preferred_element_type=F32)
             grad_mlp_in = grad_mlp[:, part]
             turned = x[part, :].astype(F32).T
@@ -507,13 +518,13 @@
             low = exact.astype(BF16)
             grad_low[micro, part, :] = low
             grad_in[part, :] = jnp.where(section == 0, exact, low.astype(F32))
-            column_sums[0] += grad_attn_in * unit
-            column_sums[1] += grad_attn_in
-            column_sums[2] += grad_mlp_in * unit
-            column_sums[3] += grad_mlp_in
+            terms = (grad_attn_in * unit, grad_attn_in, grad_mlp_in * unit, grad_mlp_in)
+            for i, term in enumerate(terms):
+                for at in range(0, NORM_CHUNK, 128):
+                    column_sums[i] += term[:, at : at + 128]
             return carry
 
-        lax.fori_loop(0, rows // ROW_CHUNK, norm_chunk, 0)
+        lax.fori_loop(0, rows // NORM_CHUNK, norm_chunk, 0)
 
         @pl.when(section == 1)
         def _():

time: 272 us -> 257 us (0.945)
  Pallas kernels: 270 us -> 255 us
    pallas_call x1, Pallas kernels: 89.7 us -> 79.4 us  [backward_call(): pl.pallas_call(functools.partial(backward_kernel, micros), out_shape=outs...]
    pallas_call x1, Pallas kernels: 45.9 us -> 39.3 us  [forward_call(): pl.pallas_call(functools.partial(forward_kernel, micros), out_shape=[jax....]
where the time goes in v4:
time: 257 us; the launch traced here: 256 us
  Pallas kernels  255 us (99%)
    pallas_call x1, Pallas kernels, reduce_call(): pl.pallas_call(functools.partial(reduce_kernel, bits, piece), out_shape=[...  127 us
    pallas_call x1, Pallas kernels, backward_call(): pl.pallas_call(functools.partial(backward_kernel, micros), out_shape=outs...  79.4 us
    pallas_call x1, Pallas kernels, forward_call(): pl.pallas_call(functools.partial(forward_kernel, micros), out_shape=[jax....  39.3 us
    pallas_call x1, Pallas kernels, finish_call(): pl.pallas_call(functools.partial(finish_kernel, grad_scale), out_shape=[j...  8.55 us

profile of v4, /device:TPU:0, one launch (start us, length us, event | category | flops | bytes accessed | tf_op | source)
XLA Modules:
  0.0 256.2 jit_solution(12104978295742321142)
XLA Ops:
  0.7 0.8 fusion
  1.4 39.3 %layer_forward.1 = (bf16[2,512,768]{2,1,0:T(8,128)(2,1)}, bf16[2,512,768]{2,1,0:T(8,128)(2,1)}, bf16[2,768,512]{2,1,0:T(8,128)(2,1)}, bf16[2,768,512]{2,1,0:T(8,...) custom-call(s32[2]{0:T(128)} %refs_0_.3, ...), custom_call_target="tpu_custom_call" | custom-call | flops 16106127360 | bytes 83886080 | tf_op jit(solution)/shard_map/layer_forward/pallas_call | solution.py:267
  40.8 79.4 %layer_backward.1 = (f32[2,512,768]{2,1,0:T(8,128)}, bf16[2,2304,512]{2,1,0:T(8,128)(2,1)}, bf16[2,512,3072]{2,1,0:T(8,128)(2,1)}, bf16[2,512,768]{2,1,0:T(8,128)(2,1)}, f32[2,16,768]{2,1,0:T(8,128)}) custom-call(s32[2]{0:T(128)} %refs_0_.3, bf16[2,512,768]{2,1,0:T(8,128)(2,1)} %bitcast.35, bf16[2,512,768]{2,1,0:T(8,128)(2,1)} %get-tuple-element.53.refs_2_, ...), custom_call_target="tpu_custom_call" | custom-call | flops 17716740096 | bytes 83886080 | tf_op jit(solution)/shard_map/layer_backward/pallas_call | solution.py:573
  120.1 127.4 %weight_gradients.1 = (bf16[2,2,48,2304]{3,2,1,0:T(8,128)(2,1)}, bf16[2,2,48,768]{3,2,1,0:T(8,128)(2,1)}, bf16[2,2,48,3072]{3,2,1,0:T(8,128)(2,1)}, bf16[4,2,2,48,768]{4,3,2,1,0:T(8,128)(2,1)}, f32[16,768]{1,0:T(8,128)}) custom-call(bf16[2,4,192,512]{3,2,1,0:T(8,128)(2,1)} %bitcast.43, bf16[2,4,4,192,512]{4,3,2,1,0:T(8,128)(2,1)} %bitcast.40, ...), custom_call_target="tpu_custom_call" | custom-call | flops 14495514624 | bytes 31457280 | tf_op jit(solution)/shard_map/weight_gradients/pallas_call | solution.py:885
  247.5 8.6 %finish.1 = (bf16[2,512,768]{2,1,0:T(8,128)(2,1)}, f32[2,512,768]{2,1,0:T(8,128)}, f32[192,2304]{1,0:T(8,128)}, f32[192,768]{1,0:T(8,128)}, f32[192,3072]{1,0:T(...) custom-call(f32[16,768]{1,0:T(8,128)} %get-tuple-element.63.refs_0_,, ...), custom_call_target="tpu_custom_call" | custom-call | tf_op jit(solution)/shard_map/finish/pallas_call | solution.py:982
  (1 shorter events, 0.0 us)

commit v5 on v4

--- a/solution.py
+++ b/solution.py
@@ -47,7 +47,7 @@
         cosine, sine, qkv_h, out_h, up_h, down_h,
         y_h, inputs_h, attn_in_h, mlp_in_h, queries_h, keys_h, values_h, probs_h, context_h, hidden_h, slope_h,
         qkv_w, out_w, up_w, down_w, x, attn_in, mlp_in, attn_in_t, mlp_in_t, heads_t, context_t, hidden_t, slope,
-        bias, total, probs, y, in_sems, out_sems, probs_sems, send_sems, recv_sems,
+        bias, total, probs, y, in_sems, out_sems, send_sems, recv_sems,
     ) = refs
     section = lax.axis_index("section")
     rows, width = attn_in.shape
@@ -92,6 +92,7 @@
             (heads_t.at[2 * width :], values_h.at[micro]),
             (context_t, context_h.at[micro]),
             (y.at[micro], y_h.at[micro]),
+            (probs, probs_h.at[micro]),
         ]
         for start in range(0, hidden_width, FF_TILE):
             part = slice(start, start + FF_TILE)
@@ -170,38 +171,28 @@
             raised = jnp.exp(scores - jnp.max(scores, axis=0, keepdims=True))
             return (raised * (1.0 / jnp.sum(raised, axis=0, keepdims=True))).astype(BF16)
 
-        def attend(head, slot):
-            at = pl.multiple_of(head * HEAD_DIM, HEAD_DIM)
-            query = heads_t[pl.ds(at, HEAD_DIM), :] * jnp.bfloat16(SCALE)
-            key = heads_t[pl.ds(width + at, HEAD_DIM), :]
-            value = heads_t[pl.ds(2 * width + at, HEAD_DIM), :]
-            early = softmax(dims_dot(key[:, :half], query[:, :half], 0, 0) + bias[:half, :half])
-            late = softmax(dims_dot(key, query[:, half:], 0, 0) + bias[:, half:])
-            probs[slot, :half, :half] = early
-            probs[slot, :, half:] = late
-            place = pl.ds(at, HEAD_DIM)
+        def scored(head):
+            at = head * HEAD_DIM
+            query = heads_t[at : at + HEAD_DIM, :] * jnp.bfloat16(SCALE)
+            key = heads_t[width + at : width + at + HEAD_DIM, :]
+            early = dims_dot(key[:, :half], query[:, :half], 0, 0) + bias[:half, :half]
+            return early, dims_dot(key, query[:, half:], 0, 0) + bias[:, half:]
+
+        settle(6, 7)
+        settle(8, 9)
+        upcoming = scored(0)
+        for head in range(HEADS):
+            early, late = upcoming
+            if head + 1 < HEADS:
+                upcoming = scored(head + 1)
+            early, late = softmax(early), softmax(late)
+            probs[head, :half, :half] = early
+            probs[head, :, half:] = late
+            place = slice(head * HEAD_DIM, (head + 1) * HEAD_DIM)
+            value = heads_t[2 * width + head * HEAD_DIM : 2 * width + (head + 1) * HEAD_DIM, :]
             context_t[place, :half] = jnp.dot(value[:, :half], early, preferred_element_type=F32).astype(BF16)
             context_t[place, half:] = jnp.dot(value, late, preferred_element_type=F32).astype(BF16)
-
-        def probs_copy(head, slot):
-            return pltpu.make_async_copy(probs.at[slot], probs_h.at[micro, head], probs_sems.at[slot])
-
-        def attend_pair(pair, carry):
-            first_slot = 2 * lax.rem(pair, 2)
-
-            @pl.when(pair >= 2)
-            def _():
-                for own_head in range(2):
-                    probs_copy(2 * pair + own_head - 4, first_slot + own_head).wait()
-
-            for own_head in range(2):
-                attend(2 * pair + own_head, first_slot + own_head)
-            for own_head in range(2):
-                probs_copy(2 * pair + own_head, first_slot + own_head).start()
-            return carry
-
-        settle(6, 7)
-        lax.fori_loop(0, HEADS // 2, attend_pair, 0)
+        store[8].start()
         store[6].start()
 
         @pl.when(micro == 0)
@@ -214,7 +205,8 @@
             + x[micro].astype(F32)
             + (out_bias[...].astype(F32) + down_bias[...].astype(F32))
         )
-        settle(7, len(store))
+        settle(7, 8)
+        settle(9, len(store))
         for start in range(0, hidden_width, FF_TILE):
             part = slice(start, start + FF_TILE)
             up = jnp.dot(mlp_in[...], up_w[:, part], preferred_element_type=F32)
@@ -224,8 +216,8 @@
             slope[:, part] = (share + up * density).astype(BF16)
             hidden_t[part, :] = hidden.T
             tile = start // FF_TILE
-            store[8 + 2 * tile].start()
             store[9 + 2 * tile].start()
+            store[10 + 2 * tile].start()
             total[...] += jnp.dot(hidden, down_w[part, :], preferred_element_type=F32)
         y[micro] = total[...].astype(BF16)
 
@@ -234,8 +226,6 @@
             hand_over(micro).start()
 
         store[7].start()
-        for head in range(HEADS - 4, HEADS):
-            probs_copy(head, head % 4).wait()
         return carry
 
     lax.fori_loop(0, micros, sentence, 0)
@@ -273,11 +263,10 @@
         + [
             pltpu.VMEM((rows, rows), F32),
             pltpu.VMEM((rows, width), F32),
-            pltpu.VMEM((4, rows, rows), BF16),
+            pltpu.VMEM((HEADS, rows, rows), BF16),
             pltpu.VMEM(wide, BF16),
             pltpu.SemaphoreType.DMA((5,)),
-            pltpu.SemaphoreType.DMA((8 + 2 * (hidden_width // FF_TILE),)),
-            pltpu.SemaphoreType.DMA((4,)),
+            pltpu.SemaphoreType.DMA((9 + 2 * (hidden_width // FF_TILE),)),
             pltpu.SemaphoreType.DMA((micros,)),
             pltpu.SemaphoreType.DMA((micros,)),
         ],
@@ -301,7 +290,7 @@
         grad_in_h, grad_heads_h, grad_up_h, grad_out_h, vectors_h,
         qkv_w, out_w, up_w, down_w, queries, keys, values, context, slope, probs, grad_out, x, grad_context,
         grad_up, grad_heads, grad_low, grad_mlp, grad_in, column_sums, vectors,
-        in_sems, stash_sems, out_sems, probs_sems, send_sems, recv_sems,
+        in_sems, stash_sems, out_sems, send_sems, recv_sems,
     ) = refs
     section = lax.axis_index("section")
     rows, width = x.shape
@@ -321,7 +310,7 @@
     def stash_loads(micro):
         pairs = (
             (slope_h, slope), (values_h, values), (context_h, context), (queries_h, queries), (keys_h, keys),
-            (inputs_h, x),
+            (probs_h, probs), (inputs_h, x),
         )
         return [
             pltpu.make_async_copy(src.at[micro], dst, stash_sems.at[i]) for i, (src, dst) in enumerate(pairs)
@@ -376,12 +365,6 @@
             def _():
                 for copy in stores(micro - 1)[first:end]:
                     copy.wait()
-
-        def probs_copy(head, slot):
-            return pltpu.make_async_copy(probs_h.at[micro, head], probs.at[slot], probs_sems.at[slot])
-
-        for head in range(2):
-            probs_copy(head, head).start()
 
         @pl.when((section == 1) & (micro == 0))
         def _():
@@ -433,7 +416,7 @@
         def _():
             upcoming[0].start()
 
-        for load in stash[1:5]:
+        for load in stash[1:6]:
             load.wait()
 
         def turn_back(grad):
@@ -446,12 +429,12 @@
             both = dims_dot(left[:, half:], late, 1, 1)
             return jnp.concatenate([both[:, :half] + dims_dot(left[:, :half], early, 1, 1), both[:, half:]], axis=1)
 
-        def attend(head, slot):
-            at = pl.multiple_of(head * HEAD_DIM, HEAD_DIM)
-            place = pl.ds(at, HEAD_DIM)
+        def attend(head):
+            at = head * HEAD_DIM
+            place = slice(at, at + HEAD_DIM)
             query, key, value, grad = queries[place, :], keys[place, :], values[place, :], grad_context[place, :]
             inner = jnp.sum(grad.astype(F32) * context[place, :].astype(F32), axis=0, keepdims=True)
-            early, late = probs[slot, :half, :half], probs[slot, :, half:]
+            early, late = probs[head, :half, :half], probs[head, :, half:]
             grad_early = dims_dot(value[:, :half], grad[:, :half], 0, 0) - inner[:, :half]
             grad_late = dims_dot(value, grad[:, half:], 0, 0) - inner[:, half:]
             grad_early = (early.astype(F32) * grad_early).astype(BF16)
@@ -466,37 +449,24 @@
                 axis=1,
             )
             grad_heads[place, :] = turn_back(grad_query * SCALE).astype(BF16)
-            grad_heads[pl.ds(width + at, HEAD_DIM), :] = turn_back(grad_key * SCALE).astype(BF16)
-            grad_heads[pl.ds(2 * width + at, HEAD_DIM), :] = grad_value.astype(BF16)
-
-        def attend_pair(pair, carry):
-            first_slot = 2 * lax.rem(pair, 2)
-
-            @pl.when(pair < HEADS // 2 - 1)
-            def _():
-                for own_head in range(2):
-                    probs_copy(2 * pair + 2 + own_head, 2 - first_slot + own_head).start()
-
-            for own_head in range(2):
-                probs_copy(2 * pair + own_head, first_slot + own_head).wait()
-            for own_head in range(2):
-                attend(2 * pair + own_head, first_slot + own_head)
-            return carry
+            grad_heads[slice(width + at, width + at + HEAD_DIM), :] = turn_back(grad_key * SCALE).astype(BF16)
+            grad_heads[slice(2 * width + at, 2 * width + at + HEAD_DIM), :] = grad_value.astype(BF16)
 
         settle(1, 2)
-        lax.fori_loop(0, HEADS // 2, attend_pair, 0)
+        for head in range(HEADS):
+            attend(head)
         store[1].start()
 
         @pl.when(micro < micros - 1)
         def _():
-            for load in upcoming[1:5]:
+            for load in upcoming[1:6]:
                 load.start()
 
         @pl.when(micro == 0)
         def _():
             loads[4].wait()
 
-        stash[5].wait()
+        stash[6].wait()
         column_sums[...] = jnp.zeros_like(column_sums)
         settle(2, 3)
 
@@ -532,7 +502,7 @@
 
         @pl.when(micro < micros - 1)
         def _():
-            upcoming[5].start()
+            upcoming[6].start()
 
         store[2].start()
         columns = [jnp.sum(column_sums[i], axis=1, keepdims=True) for i in range(4)]
@@ -585,7 +555,7 @@
             pltpu.VMEM(tall, BF16),
             pltpu.VMEM(tall, BF16),
             pltpu.VMEM((rows, hidden_width), BF16),
-            pltpu.VMEM((4, rows, rows), BF16),
+            pltpu.VMEM((HEADS, rows, rows), BF16),
             pltpu.VMEM(wide, BF16),
             pltpu.VMEM((rows, width), BF16),
             pltpu.VMEM(tall, BF16),
@@ -597,9 +567,8 @@
             pltpu.VMEM((4, width, 128), F32),
             pltpu.VMEM((vector_rows, width), F32),
             pltpu.SemaphoreType.DMA((5,)),
-            pltpu.SemaphoreType.DMA((6,)),
+            pltpu.SemaphoreType.DMA((7,)),
             pltpu.SemaphoreType.DMA((4 + hidden_width // FF_TILE,)),
-            pltpu.SemaphoreType.DMA((4,)),
             pltpu.SemaphoreType.DMA((micros,)),
             pltpu.SemaphoreType.DMA((micros,)),
         ],
@@ -818,7 +787,7 @@
 
     lags = [0]
     for stage in range(n_steps):
-        lags.append(lags[-1] + (4 if stage == 0 else 2))
+        lags.append(lags[-1] + 3)
 
     def turn(t, carry):
         for at, group in zip((down_at, up_at, qkv_at), copies[1:]):

time: 257 us -> 243 us (0.946)
  Pallas kernels: 255 us -> 241 us
    pallas_call x1, Pallas kernels: 79.4 us -> 70.2 us  [backward_call(): pl.pallas_call(functools.partial(backward_kernel, micros), out_shape=outs...]
    pallas_call x1, Pallas kernels: 39.3 us -> 34 us  [forward_call(): pl.pallas_call(functools.partial(forward_kernel, micros), out_shape=[jax....]
where the time goes in v5:
time: 243 us
  Pallas kernels  241 us (99%)
    pallas_call x1, Pallas kernels, reduce_call(): pl.pallas_call(functools.partial(reduce_kernel, bits, piece), out_shape=[...  128 us
    pallas_call x1, Pallas kernels, backward_call(): pl.pallas_call(functools.partial(backward_kernel, micros), out_shape=outs...  70.2 us
    pallas_call x1, Pallas kernels, forward_call(): pl.pallas_call(functools.partial(forward_kernel, micros), out_shape=[jax....  34 us
    pallas_call x1, Pallas kernels, finish_call(): pl.pallas_call(functools.partial(finish_kernel, grad_scale), out_shape=[j...  8.55 us

profile of v5, /device:TPU:0, one launch (start us, length us, event | category | flops | bytes accessed | tf_op | source)
XLA Modules:
  0.0 242.8 jit_solution(14064397167530017981)
XLA Ops:
  0.7 0.8 fusion
  1.4 34.0 %layer_forward.1 = (bf16[2,512,768]{2,1,0:T(8,128)(2,1)}, bf16[2,512,768]{2,1,0:T(8,128)(2,1)}, bf16[2,768,512]{2,1,0:T(8,128)(2,1)}, bf16[2,768,512]{2,1,0:T(8,...) custom-call(s32[2]{0:T(128)} %refs_0_.3, ...), custom_call_target="tpu_custom_call" | custom-call | flops 16106127360 | bytes 83886080 | tf_op jit(solution)/shard_map/layer_forward/pallas_call | solution.py:257
  35.4 70.2 %layer_backward.1 = (f32[2,512,768]{2,1,0:T(8,128)}, bf16[2,2304,512]{2,1,0:T(8,128)(2,1)}, bf16[2,512,3072]{2,1,0:T(8,128)(2,1)}, bf16[2,512,768]{2,1,0:T(8,128)(2,1)}, f32[2,16,768]{2,1,0:T(8,128)}) custom-call(s32[2]{0:T(128)} %refs_0_.3, bf16[2,512,768]{2,1,0:T(8,128)(2,1)} %bitcast.35, bf16[2,512,768]{2,1,0:T(8,128)(2,1)} %get-tuple-element.53.refs_2_, ...), custom_call_target="tpu_custom_call" | custom-call | flops 17716740096 | bytes 83886080 | tf_op jit(solution)/shard_map/layer_backward/pallas_call | solution.py:543
  105.7 128.4 %weight_gradients.1 = (bf16[2,2,48,2304]{3,2,1,0:T(8,128)(2,1)}, bf16[2,2,48,768]{3,2,1,0:T(8,128)(2,1)}, bf16[2,2,48,3072]{3,2,1,0:T(8,128)(2,1)}, bf16[4,2,2,48,768]{4,3,2,1,0:T(8,128)(2,1)}, f32[16,768]{1,0:T(8,128)}) custom-call(bf16[2,4,192,512]{3,2,1,0:T(8,128)(2,1)} %bitcast.43, bf16[2,4,4,192,512]{4,3,2,1,0:T(8,128)(2,1)} %bitcast.40, ...), custom_call_target="tpu_custom_call" | custom-call | flops 14495514624 | bytes 31457280 | tf_op jit(solution)/shard_map/weight_gradients/pallas_call | solution.py:854
  234.1 8.6 %finish.1 = (bf16[2,512,768]{2,1,0:T(8,128)(2,1)}, f32[2,512,768]{2,1,0:T(8,128)}, f32[192,2304]{1,0:T(8,128)}, f32[192,768]{1,0:T(8,128)}, f32[192,3072]{1,0:T(...) custom-call(f32[16,768]{1,0:T(8,128)} %get-tuple-element.63.refs_0_,, ...), custom_call_target="tpu_custom_call" | custom-call | tf_op jit(solution)/shard_map/finish/pallas_call | solution.py:951
  (1 shorter events, 0.0 us)

commit v6 on v5

--- a/solution.py
+++ b/solution.py
@@ -2,6 +2,7 @@
 
 import jax
 import jax.numpy as jnp
+import numpy as np
 from jax import lax
 from jax.experimental import pallas as pl
 from jax.experimental.pallas import tpu as pltpu
@@ -111,20 +112,21 @@
                 for copy in stores(micro - 1)[first:end]:
                     copy.wait()
 
-        @pl.when((section == 0) & (micro == 0))
-        def _():
-            loads[0].wait()
-
-        @pl.when(section == 1)
-        def _():
-            hand_over(micro).wait_recv()
-
         length = lengths[micro]
         key_ids = lax.broadcasted_iota(jnp.int32, (rows, rows), 0)
         query_ids = lax.broadcasted_iota(jnp.int32, (rows, rows), 1)
         bias[...] = jnp.where((key_ids <= query_ids) & (key_ids < length), 0.0, MASKED)
 
         settle(0, 3)
+
+        @pl.when((section == 0) & (micro == 0))
+        def _():
+            loads[0].wait()
+
+        @pl.when(section == 1)
+        def _():
+            hand_over(micro).wait_recv()
+
         store[0].start()
         for start in range(0, rows, ROW_CHUNK):
             part = slice(start, start + ROW_CHUNK)
@@ -915,8 +917,9 @@
     ready = (*held[:2], *wide)
     loads = [pltpu.make_async_copy(src, dst, in_sems.at[i]) for i, (src, dst) in enumerate(zip(sources, held))]
     stores = [pltpu.make_async_copy(src, dst, out_sems.at[i]) for i, (src, dst) in enumerate(zip(ready, targets))]
-    for load in loads:
-        load.start()
+    order = (1, 0, 3, 2, 4, 5)
+    for i in order:
+        loads[i].start()
     devices = lax.axis_size("dp")
     mine = lax.axis_index("dp")
     width = vectors.shape[1]
@@ -934,11 +937,11 @@
                     out[:, filled : filled + count] = piece * grad_scale
                     filled += count
 
-    for i, (load, store) in enumerate(zip(loads, stores)):
-        load.wait()
+    for i in order:
+        loads[i].wait()
         if i >= 2:
             wide[i - 2][...] = held[i][...].astype(F32) * grad_scale
-        store.start()
+        stores[i].start()
     for store in stores:
         store.wait()
 
@@ -968,10 +971,11 @@
 
 
 def rotary_tables(seq_len):
-    positions = jnp.arange(seq_len, dtype=F32)
-    inverse = 1.0 / ROTARY_BASE ** (jnp.arange(0, ROTARY, 2, dtype=F32) / ROTARY)
+    positions = np.arange(seq_len, dtype=np.float32)
+    exponents = np.arange(0, ROTARY, 2, dtype=np.float32) / np.float32(ROTARY)
+    inverse = np.float32(1.0) / np.float32(ROTARY_BASE) ** exponents
     angles = inverse[:, None] * positions[None, :]
-    return jnp.cos(angles), jnp.sin(angles)
+    return jnp.asarray(np.cos(angles)), jnp.asarray(np.sin(angles))
 
 
 def summed(share):

time: 243 us -> 242 us (level)
  no operation moved by 1% of the time
where the time goes in v6:
time: 242 us; the launch traced here: 241 us
  Pallas kernels  241 us (100%)
    pallas_call x1, Pallas kernels, reduce_call(): pl.pallas_call(functools.partial(reduce_kernel, bits, piece), out_shape=[...  128 us
    pallas_call x1, Pallas kernels, backward_call(): pl.pallas_call(functools.partial(backward_kernel, micros), out_shape=outs...  70.2 us
    pallas_call x1, Pallas kernels, forward_call(): pl.pallas_call(functools.partial(forward_kernel, micros), out_shape=[jax....  34.2 us
    pallas_call x1, Pallas kernels, finish_call(): pl.pallas_call(functools.partial(finish_kernel, grad_scale), out_shape=[j...  7.79 us

profile of v6, /device:TPU:0, one launch (start us, length us, event | category | flops | bytes accessed | tf_op | source)
XLA Modules:
  0.0 241.4 jit_solution(11711146396989002157)
XLA Ops:
  0.6 34.2 %layer_forward.1 = (bf16[2,512,768]{2,1,0:T(8,128)(2,1)}, bf16[2,512,768]{2,1,0:T(8,128)(2,1)}, bf16[2,768,512]{2,1,0:T(8,128)(2,1)}, bf16[2,768,512]{2,1,0:T(8,...) custom-call(s32[2]{0:T(128)} %refs_0_.3, ...), custom_call_target="tpu_custom_call" | custom-call | flops 16106127360 | bytes 83886080 | tf_op jit(solution)/shard_map/layer_forward/pallas_call | solution.py:259
  34.9 70.2 %layer_backward.1 = (f32[2,512,768]{2,1,0:T(8,128)}, bf16[2,2304,512]{2,1,0:T(8,128)(2,1)}, bf16[2,512,3072]{2,1,0:T(8,128)(2,1)}, bf16[2,512,768]{2,1,0:T(8,128)(2,1)}, f32[2,16,768]{2,1,0:T(8,128)}) custom-call(s32[2]{0:T(128)} %refs_0_.3, bf16[2,512,768]{2,1,0:T(8,128)(2,1)} %bitcast.35, bf16[2,512,768]{2,1,0:T(8,128)(2,1)} %get-tuple-element.53.refs_2_, ...), custom_call_target="tpu_custom_call" | custom-call | flops 17716740096 | bytes 83886080 | tf_op jit(solution)/shard_map/layer_backward/pallas_call | solution.py:545
  105.1 128.4 %weight_gradients.1 = (bf16[2,2,48,2304]{3,2,1,0:T(8,128)(2,1)}, bf16[2,2,48,768]{3,2,1,0:T(8,128)(2,1)}, bf16[2,2,48,3072]{3,2,1,0:T(8,128)(2,1)}, bf16[4,2,2,48,768]{4,3,2,1,0:T(8,128)(2,1)}, f32[16,768]{1,0:T(8,128)}) custom-call(bf16[2,4,192,512]{3,2,1,0:T(8,128)(2,1)} %bitcast.43, bf16[2,4,4,192,512]{4,3,2,1,0:T(8,128)(2,1)} %bitcast.40, ...), custom_call_target="tpu_custom_call" | custom-call | flops 14495514624 | bytes 31457280 | tf_op jit(solution)/shard_map/weight_gradients/pallas_call | solution.py:856
  233.5 7.8 %finish.1 = (bf16[2,512,768]{2,1,0:T(8,128)(2,1)}, f32[2,512,768]{2,1,0:T(8,128)}, f32[192,2304]{1,0:T(8,128)}, f32[192,768]{1,0:T(8,128)}, f32[192,3072]{1,0:T(...) custom-call(f32[16,768]{1,0:T(8,128)} %get-tuple-element.63.refs_0_,, ...), custom_call_target="tpu_custom_call" | custom-call | tf_op jit(solution)/shard_map/finish/pallas_call | solution.py:954

commit v7 on v6

--- a/solution.py
+++ b/solution.py
@@ -23,7 +23,7 @@
 ANY = pl.BlockSpec(memory_space=pl.ANY)
 VMEM = pl.BlockSpec(memory_space=pltpu.VMEM)
 SMEM = pl.BlockSpec(memory_space=pltpu.SMEM)
-ROW_CHUNK = 128
+ROW_CHUNK = 256
 NORM_CHUNK = 256
 QKV_TILE = 256
 FF_TILE = 768
@@ -101,6 +101,11 @@
             pairs.append((slope.at[:, part], slope_h.at[micro, :, part]))
         return [pltpu.make_async_copy(src, dst, out_sems.at[i]) for i, (src, dst) in enumerate(pairs)]
 
+    @pl.when(section == 1)
+    def _():
+        for load in loads[2:]:
+            load.start()
+
     pl.semaphore_wait(barrier, 1)
 
     def sentence(micro, carry):
@@ -145,6 +150,9 @@
         @pl.when(micro == 0)
         def _():
             loads[1].wait()
+
+        @pl.when((micro == 0) & (section == 0))
+        def _():
             for load in loads[2:]:
                 load.start()
 

time: 242 us -> 242 us (level)
  no operation moved by 1% of the time
where the time goes in v7:
time: 242 us; the launch traced here: 241 us
  Pallas kernels  240 us (99%)
    pallas_call x1, Pallas kernels, reduce_call(): pl.pallas_call(functools.partial(reduce_kernel, bits, piece), out_shape=[...  128 us
    pallas_call x1, Pallas kernels, backward_call(): pl.pallas_call(functools.partial(backward_kernel, micros), out_shape=outs...  70.1 us
    pallas_call x1, Pallas kernels, forward_call(): pl.pallas_call(functools.partial(forward_kernel, micros), out_shape=[jax....  34.1 us
    pallas_call x1, Pallas kernels, finish_call(): pl.pallas_call(functools.partial(finish_kernel, grad_scale), out_shape=[j...  7.79 us

profile of v7, /device:TPU:0, one launch (start us, length us, event | category | flops | bytes accessed | tf_op | source)
XLA Modules:
  0.0 241.2 jit_solution(3215863158295972534)
XLA Ops:
  0.6 34.1 %layer_forward.1 = (bf16[2,512,768]{2,1,0:T(8,128)(2,1)}, bf16[2,512,768]{2,1,0:T(8,128)(2,1)}, bf16[2,768,512]{2,1,0:T(8,128)(2,1)}, bf16[2,768,512]{2,1,0:T(8,...) custom-call(s32[2]{0:T(128)} %refs_0_.3, ...), custom_call_target="tpu_custom_call" | custom-call | flops 16106127360 | bytes 83886080 | tf_op jit(solution)/shard_map/layer_forward/pallas_call | solution.py:267
  34.7 70.1 %layer_backward.1 = (f32[2,512,768]{2,1,0:T(8,128)}, bf16[2,2304,512]{2,1,0:T(8,128)(2,1)}, bf16[2,512,3072]{2,1,0:T(8,128)(2,1)}, bf16[2,512,768]{2,1,0:T(8,128)(2,1)}, f32[2,16,768]{2,1,0:T(8,128)}) custom-call(s32[2]{0:T(128)} %refs_0_.3, bf16[2,512,768]{2,1,0:T(8,128)(2,1)} %bitcast.35, bf16[2,512,768]{2,1,0:T(8,128)(2,1)} %get-tuple-element.53.refs_2_, ...), custom_call_target="tpu_custom_call" | custom-call | flops 17716740096 | bytes 83886080 | tf_op jit(solution)/shard_map/layer_backward/pallas_call | solution.py:553
  104.8 128.4 %weight_gradients.1 = (bf16[2,2,48,2304]{3,2,1,0:T(8,128)(2,1)}, bf16[2,2,48,768]{3,2,1,0:T(8,128)(2,1)}, bf16[2,2,48,3072]{3,2,1,0:T(8,128)(2,1)}, bf16[4,2,2,48,768]{4,3,2,1,0:T(8,128)(2,1)}, f32[16,768]{1,0:T(8,128)}) custom-call(bf16[2,4,192,512]{3,2,1,0:T(8,128)(2,1)} %bitcast.43, bf16[2,4,4,192,512]{4,3,2,1,0:T(8,128)(2,1)} %bitcast.40, ...), custom_call_target="tpu_custom_call" | custom-call | flops 14495514624 | bytes 31457280 | tf_op jit(solution)/shard_map/weight_gradients/pallas_call | solution.py:864
  233.2 7.8 %finish.1 = (bf16[2,512,768]{2,1,0:T(8,128)(2,1)}, f32[2,512,768]{2,1,0:T(8,128)}, f32[192,2304]{1,0:T(8,128)}, f32[192,768]{1,0:T(8,128)}, f32[192,3072]{1,0:T(...) custom-call(f32[16,768]{1,0:T(8,128)} %get-tuple-element.63.refs_0_,, ...), custom_call_target="tpu_custom_call" | custom-call | tf_op jit(solution)/shard_map/finish/pallas_call | solution.py:962
